TPU v7x, 128 devices: a whole 4x4x4 slice. The times are simulated.
128 devices in a mesh: dp: 8 (over x_hi, z), context: 16 (over x_lo, y, core).
Axes of the slice: x: 4 (x_hi: 2, x_lo: 2; x = x_hi * 2 + x_lo), y: 4, z: 4, core: 2. Of those that a mesh axis runs over, the one named last changes fastest.
Arguments:
- queries: bfloat16 [65536, 1024], P(('dp', 'context')), parts along dimension 0, may hold values from -110 to 110
- key_rows: bfloat16 [65536, 128], P(('dp', 'context')), parts along dimension 0, may hold values from -5 to 5
- values: bfloat16 [65536, 128], P(('dp', 'context')), parts along dimension 0, may hold values from -6 to 6
- out_grad: bfloat16 [65536, 1024], P(('dp', 'context')), parts along dimension 0, may hold values from -6 to 6
- lengths: int32 [128], P('dp'), parts along dimension 0, may hold values from 1 to 4096, 8192 in all
- block_owner: int32 [1024], P('dp'), parts along dimension 0, may hold values from 0 to 15, as said below
Outputs:
- attn_out: bfloat16 [65536, 1024], P(('dp', 'context')), parts along dimension 0
- query_grad: bfloat16 [65536, 1024], P(('dp', 'context')), parts along dimension 0
- key_grad: bfloat16 [65536, 128], P(('dp', 'context')), parts along dimension 0
- value_grad: bfloat16 [65536, 128], P(('dp', 'context')), parts along dimension 0
- pair_count: float32 [128], P(('dp', 'context')), parts along dimension 0
There are 8 independent parts, one for each index of `dp`. A program takes and returns all parts, laid end to end along the dimension named above; each array names one. Nothing has to cross between parts.
Inputs may be any that keep to these rules, and one draw needn't show every extreme that they name: Each pack's lengths sum to 8192; one document has exactly 4096 tokens. `block_owner`: each rank is assigned exactly 8 blocks, and at most one of the 8 blocks of any one rank's own rows.
All inputs are finite; a program needn't handle non-finite values.
Results may differ from a plain program's by a relative error of at most 0.035.
Values may be sent and summed in bfloat16 or wider, within the bound.
A program may use at most 64 MiB of HBM per device.

v0:
```python
import math

import jax
import jax.numpy as jnp
from jax import lax
from jax.sharding import PartitionSpec as P

NEG_FILL = -1e30


def doc_starts(lengths, total_rows):
    doc_ends = jnp.cumsum(lengths)
    position = jnp.arange(total_rows, dtype=jnp.int32)
    passed = doc_ends[None, :] <= position[:, None]
    starts = jnp.sum(jnp.where(passed, lengths[None, :], 0), axis=1)
    return (position, starts)


def attend(query_rows, grad_rows, block_first, key_all, value_all, starts, head_count, tile_rows):
    row_count, feature_width = query_rows.shape
    total_keys, head_dim = key_all.shape
    score_scale = 1.0 / math.sqrt(head_dim)
    block_count = block_first.shape[0]
    block_rows = row_count // block_count
    flat_rows = block_rows * head_count

    def one_block(block_idx, state_four):
        attn_acc, query_acc, key_acc, value_acc = state_four
        first = lax.dynamic_index_in_dim(block_first, block_idx, 0, keepdims=False)
        row_begin = block_idx * block_rows
        query_tile = lax.dynamic_slice_in_dim(query_rows, row_begin, block_rows, 0).reshape(
            flat_rows, head_dim
        )
        grad_tile = lax.dynamic_slice_in_dim(grad_rows, row_begin, block_rows, 0).reshape(
            flat_rows, head_dim
        )
        row_pos = first + jnp.arange(block_rows, dtype=jnp.int32)
        row_start = lax.dynamic_slice_in_dim(starts, first, block_rows, 0)
        tile_low = row_start[0] // tile_rows
        tile_high = (first + block_rows - 1) // tile_rows + 1

        def tile_scores(tile_idx):
            key_begin = (tile_idx * tile_rows).astype(jnp.int32)
            key_tile = lax.dynamic_slice_in_dim(key_all, key_begin, tile_rows, 0)
            value_tile = lax.dynamic_slice_in_dim(value_all, key_begin, tile_rows, 0)
            pos_tile = key_begin + jnp.arange(tile_rows, dtype=jnp.int32)
            allowed = (pos_tile[None, :] >= row_start[:, None]) & (
                pos_tile[None, :] <= row_pos[:, None]
            )
            scores = lax.dot_general(
                query_tile, key_tile, (((1,), (1,)), ((), ())), preferred_element_type=jnp.float32
            )
            scores = scores.reshape(block_rows, head_count, tile_rows) * score_scale
            return (key_begin, key_tile, value_tile, allowed[:, None, :], scores)

        def peak_pass(tile_idx, stats):
            row_peak, exp_total = stats
            _, _, _, allowed, scores = tile_scores(tile_idx)
            tile_peak = jnp.max(jnp.where(allowed, scores, NEG_FILL), axis=-1)
            new_peak = jnp.maximum(row_peak, tile_peak)
            tile_total = jnp.sum(
                jnp.where(allowed, jnp.exp(scores - new_peak[..., None]), 0.0), axis=-1
            )
            return (new_peak, exp_total * jnp.exp(row_peak - new_peak) + tile_total)

        stats_start = (
            jnp.full((block_rows, head_count), NEG_FILL, jnp.float32),
            jnp.zeros((block_rows, head_count), jnp.float32),
        )
        row_peak, exp_total = lax.fori_loop(tile_low, tile_high, peak_pass, stats_start)
        log_total = row_peak + jnp.log(exp_total)

        def tile_weights(tile_idx):
            key_begin, key_tile, value_tile, allowed, scores = tile_scores(tile_idx)
            weights = jnp.where(allowed, jnp.exp(scores - log_total[..., None]), 0.0)
            return (key_begin, key_tile, value_tile, weights)

        def output_pass(tile_idx, out_acc):
            _, _, value_tile, weights = tile_weights(tile_idx)
            weights_low = weights.astype(jnp.bfloat16).reshape(flat_rows, tile_rows)
            return out_acc + jnp.dot(weights_low, value_tile, preferred_element_type=jnp.float32)

        out_wide = lax.fori_loop(
            tile_low, tile_high, output_pass, jnp.zeros((flat_rows, head_dim), jnp.float32)
        )
        attn_flat = out_wide.astype(jnp.bfloat16)
        grad_dot = jnp.sum(grad_tile.astype(jnp.float32) * attn_flat.astype(jnp.float32), axis=-1)
        grad_dot = grad_dot.reshape(block_rows, head_count)

        def grad_pass(tile_idx, grads_three):
            query_sum, key_now, value_now = grads_three
            key_begin, key_tile, value_tile, weights = tile_weights(tile_idx)
            weights_low = weights.astype(jnp.bfloat16).reshape(flat_rows, tile_rows)
            grad_weights = lax.dot_general(
                grad_tile, value_tile, (((1,), (1,)), ((), ())), preferred_element_type=jnp.float32
            )
            grad_weights = grad_weights.reshape(block_rows, head_count, tile_rows)
            grad_scores = (weights * (grad_weights - grad_dot[..., None])).astype(jnp.bfloat16)
            grad_scores = grad_scores.reshape(flat_rows, tile_rows)
            query_sum = query_sum + jnp.dot(
                grad_scores, key_tile, preferred_element_type=jnp.float32
            )
            key_term = lax.dot_general(
                grad_scores,
                query_tile,
                (((0,), (0,)), ((), ())),
                preferred_element_type=jnp.float32,
            )
            value_term = lax.dot_general(
                weights_low, grad_tile, (((0,), (0,)), ((), ())), preferred_element_type=jnp.float32
            )
            key_old = lax.dynamic_slice_in_dim(key_now, key_begin, tile_rows, 0)
            value_old = lax.dynamic_slice_in_dim(value_now, key_begin, tile_rows, 0)
            key_now = lax.dynamic_update_slice_in_dim(key_now, key_old + key_term, key_begin, 0)
            value_now = lax.dynamic_update_slice_in_dim(
                value_now, value_old + value_term, key_begin, 0
            )
            return (query_sum, key_now, value_now)

        query_sum, key_acc, value_acc = lax.fori_loop(
            tile_low,
            tile_high,
            grad_pass,
            (jnp.zeros((flat_rows, head_dim), jnp.float32), key_acc, value_acc),
        )
        query_part = (
            (query_sum * score_scale).astype(jnp.bfloat16).reshape(block_rows, feature_width)
        )
        attn_acc = lax.dynamic_update_slice_in_dim(
            attn_acc, attn_flat.reshape(block_rows, feature_width), row_begin, 0
        )
        query_acc = lax.dynamic_update_slice_in_dim(query_acc, query_part, row_begin, 0)
        return (attn_acc, query_acc, key_acc, value_acc)

    start_state = (
        jnp.zeros((row_count, feature_width), jnp.bfloat16),
        jnp.zeros((row_count, feature_width), jnp.bfloat16),
        jnp.zeros((total_keys, head_dim), jnp.float32),
        jnp.zeros((total_keys, head_dim), jnp.float32),
    )
    attn_acc, query_acc, key_acc, value_acc = lax.fori_loop(0, block_count, one_block, start_state)
    return (attn_acc, query_acc, key_acc * score_scale, value_acc)


def body(queries, key_rows, values, out_grad, lengths, block_owner):
    rank_count = lax.axis_size("context")
    rank_id = lax.axis_index("context")
    local_rows, feature_width = queries.shape
    head_dim = key_rows.shape[1]
    head_count = feature_width // head_dim
    block_total = block_owner.shape[0]
    per_rank = block_total // rank_count
    block_rows = local_rows // per_rank
    tile_rows = min(512, local_rows)
    position, starts = doc_starts(lengths, local_rows * rank_count)
    row_total = (position - starts + 1).astype(jnp.float32)
    block_pairs = jnp.sum(row_total.reshape(block_total, block_rows), axis=1)
    pair_count = jnp.sum(jnp.where(block_owner == rank_id, block_pairs, 0.0)).reshape(1)
    source_plan = lax.dynamic_slice_in_dim(block_owner, rank_id * per_rank, per_rank)
    rank_line = jnp.arange(rank_count, dtype=jnp.int32)
    send_route = (source_plan[None, :] == rank_line[:, None]).astype(jnp.bfloat16)
    query_blocks = queries.reshape(per_rank, block_rows, feature_width)
    grad_blocks = out_grad.reshape(per_rank, block_rows, feature_width)
    send_query = jnp.einsum(
        "dj,jbf->dbf", send_route, query_blocks, preferred_element_type=jnp.float32
    )
    send_query = send_query.astype(jnp.bfloat16).reshape(rank_count * block_rows, feature_width)
    send_grad = jnp.einsum(
        "dj,jbf->dbf", send_route, grad_blocks, preferred_element_type=jnp.float32
    )
    send_grad = send_grad.astype(jnp.bfloat16).reshape(rank_count * block_rows, feature_width)
    got_query, got_grad = (
        lax.all_to_all(send_query, "context", split_axis=0, concat_axis=0, tiled=True),
        lax.all_to_all(send_grad, "context", split_axis=0, concat_axis=0, tiled=True),
    )
    owner_table = block_owner.reshape(rank_count, per_rank)
    owner_hit = owner_table == rank_id
    has_block = jnp.any(owner_hit, axis=1)
    slot_rank = jnp.cumsum(has_block.astype(jnp.int32)) - 1
    slot_line = jnp.arange(per_rank, dtype=jnp.int32)
    slot_pick = has_block[None, :] & (slot_rank[None, :] == slot_line[:, None])
    block_ident = (
        jnp.sum(jnp.where(owner_hit, slot_line[None, :], 0), axis=1) + rank_line * per_rank
    )
    chosen_ident = jnp.sum(jnp.where(slot_pick, block_ident[None, :], 0), axis=1)
    pick_low = slot_pick.astype(jnp.bfloat16)
    query_take = jnp.einsum(
        "ks,sbf->kbf",
        pick_low,
        got_query.reshape(rank_count, block_rows, feature_width),
        preferred_element_type=jnp.float32,
    )
    query_take = query_take.astype(jnp.bfloat16).reshape(local_rows, feature_width)
    grad_take = jnp.einsum(
        "ks,sbf->kbf",
        pick_low,
        got_grad.reshape(rank_count, block_rows, feature_width),
        preferred_element_type=jnp.float32,
    )
    grad_take = grad_take.astype(jnp.bfloat16).reshape(local_rows, feature_width)
    plan_first = chosen_ident * block_rows
    key_all, value_all = (
        lax.all_gather(key_rows, "context", axis=0, tiled=True),
        lax.all_gather(values, "context", axis=0, tiled=True),
    )
    attn_take, query_grad_take, key_term, value_term = attend(
        query_take, grad_take, plan_first, key_all, value_all, starts, head_count, tile_rows
    )
    back_attn = jnp.einsum(
        "ks,kbf->sbf",
        pick_low,
        attn_take.reshape(per_rank, block_rows, feature_width),
        preferred_element_type=jnp.float32,
    )
    back_attn = back_attn.astype(jnp.bfloat16).reshape(rank_count * block_rows, feature_width)
    back_grad = jnp.einsum(
        "ks,kbf->sbf",
        pick_low,
        query_grad_take.reshape(per_rank, block_rows, feature_width),
        preferred_element_type=jnp.float32,
    )
    back_grad = back_grad.astype(jnp.bfloat16).reshape(rank_count * block_rows, feature_width)
    got_attn, got_query_grad = (
        lax.all_to_all(back_attn, "context", split_axis=0, concat_axis=0, tiled=True),
        lax.all_to_all(back_grad, "context", split_axis=0, concat_axis=0, tiled=True),
    )
    attn_out = jnp.einsum(
        "dj,dbf->jbf",
        send_route,
        got_attn.reshape(rank_count, block_rows, feature_width),
        preferred_element_type=jnp.float32,
    )
    attn_out = attn_out.astype(jnp.bfloat16).reshape(local_rows, feature_width)
    query_grad = jnp.einsum(
        "dj,dbf->jbf",
        send_route,
        got_query_grad.reshape(rank_count, block_rows, feature_width),
        preferred_element_type=jnp.float32,
    )
    query_grad = query_grad.astype(jnp.bfloat16).reshape(local_rows, feature_width)
    key_sum, value_sum = (
        lax.psum_scatter(key_term, "context", scatter_dimension=0, tiled=True),
        lax.psum_scatter(value_term, "context", scatter_dimension=0, tiled=True),
    )
    return (
        attn_out,
        query_grad,
        key_sum.astype(jnp.bfloat16),
        value_sum.astype(jnp.bfloat16),
        pair_count,
    )


def solution(mesh):
    in_specs = (
        P(("dp", "context"), None),
        P(("dp", "context"), None),
        P(("dp", "context"), None),
        P(("dp", "context"), None),
        P("dp"),
        P("dp"),
    )
    out_specs = (
        P(("dp", "context"), None),
        P(("dp", "context"), None),
        P(("dp", "context"), None),
        P(("dp", "context"), None),
        P(("dp", "context")),
    )
    return jax.shard_map(body, mesh=mesh, in_specs=in_specs, out_specs=out_specs, check_vma=False)
```

profile of v0, /device:TPU:96, one launch (start us, length us, event | category | flops | bytes accessed | tf_op | source)
XLA Modules:
  0.0 960.5 jit_solution(10136025472506204103)
XLA Ops:
  9.6 2.5 copy.72
  12.1 5.5 all-to-all-start
  18.3 2.1 convolution_convert_fusion.2
  20.5 2.5 copy.76
  23.0 30.4 %all-to-all-done = bf16[16,64,1024]{2,1,0:T(8,128)(2,1)S(1)} async-done(((bf16[16,64,1024]{2,1,0:T(8,128)(2,1)}), bf16[16,64,1024]{2,1,0:T(8,128)(2,1)S(1)}, u32[]{:S(2)}, u32[]{:S(2)}) %all-to-all-start) | async-done | bytes 2097184 | tf_op jit(solution)/shard_map/all_to_all | solution.py:173
  53.3 4.4 all-to-all-start.1
  62.9 28.1 %all-to-all-done.1 = bf16[16,64,1024]{2,1,0:T(8,128)(2,1)} async-done(((bf16[16,64,1024]{2,1,0:T(8,128)(2,1)}), bf16[16,64,1024]{2,1,0:T(8,128)(2,1)}, u32[]{:S(2)}, u32[]{:S(2)}) %all-to-all-start.1) | async-done | bytes 2097184 | tf_op jit(solution)/shard_map/all_to_all | solution.py:174
  90.9 2.9 fusion.53
  95.3 9.7 %all-gather.5.cloned.1.call-done = bf16[8192,128]{1,0:T(8,128)(2,1)} async-done(((bf16[512,128]{1,0:T(8,128)(2,1)}), bf16[8192,128]{1,0:T(8,128)(2,1)}) %all-gather.5.cloned.1.call-update) | async-done | bytes 2097168 | tf_op jit(solution)/shard_map/all_gather | solution.py:204
  107.3 2.2 broadcast.235.clone
  109.5 2.2 broadcast.235
  111.8 400.2 %while.182 = (s32[]{:T(128)}, bf16[512,1024]{1,0:T(8,128)(2,1)}, bf16[512,1024]{1,0:T(8,128)(2,1)}, f32[8192,128]{1,0:T(8,128)}, f32[8192,128]{1,0:T(8,128)}, /*...) while((s32[]{:T(128)}, bf16[512,1024]{1,0:T(8,128)(2,1)}, ...), condition=%wide.region_16.17_spmd, body=%wide.region_6.16_spmd.sunk | while | flops 542345984 | bytes 17720784 | solution.py:141
  116.4 3.1 while.183
  120.1 2.9 while.184
  123.9 8.9 while.185
  138.3 6.2 while.183
  145.1 5.8 while.184
  151.9 17.9 %while.185 = (s32[]{:T(128)}, f32[512,128]{1,0:T(8,128)S(1)}, f32[8192,128]{1,0:T(8,128)}, f32[8192,128]{1,0:T(8,128)}, s32[]{:T(128)}, /*index=5*/s32[64]{0:T(1...) while((s32[]{:T(128)}, f32[512,128]{1,0:T(8,128)S(1)}, ...), condition=%wide.wide.region_15.15_spmd.clone, body=%wide.wide.region_14.14_spmd.clone.sunk | while | flops 337674816 | bytes 8332271 | solution.py:120
  175.1 9.3 while.183
  185.1 8.7 while.184
  194.8 26.9 %while.185 = (s32[]{:T(128)}, f32[512,128]{1,0:T(8,128)S(1)}, f32[8192,128]{1,0:T(8,128)}, f32[8192,128]{1,0:T(8,128)}, s32[]{:T(128)}, /*index=5*/s32[64]{0:T(1...) while((s32[]{:T(128)}, f32[512,128]{1,0:T(8,128)S(1)}, ...), condition=%wide.wide.region_15.15_spmd.clone, body=%wide.wide.region_14.14_spmd.clone.sunk | while | flops 337674816 | bytes 8332271 | solution.py:120
  217.7 2.0 fusion.144
  227.0 15.6 %while.183 = (s32[]{:T(128)}, f32[64,8]{1,0:T(8,128)S(1)}, f32[64,8]{1,0:T(8,128)S(1)}, s32[]{:T(128)}, s32[64]{0:T(128)S(1)}, /*index=5*/bf16[8192,128]{1,0:T(8...) while((s32[]{:T(128)}, f32[64,8]{1,0:T(8,128)S(1)}, ...), condition=%wide.region_10.10_spmd.clone, body=%wide.region_7.9_spmd.clone.sunk | while | flops 68781640 | bytes 3779503 | solution.py:70
  243.3 14.5 %while.184 = (s32[]{:T(128)}, f32[512,128]{1,0:T(8,128)S(1)}, s32[]{:T(128)}, s32[64]{0:T(128)S(1)}, bf16[8192,128]{1,0:T(8,128)(2,1)}, /*index=5*/bf16[512,128]...) while((s32[]{:T(128)}, f32[512,128]{1,0:T(8,128)S(1)}, ...), condition=%wide.wide.region_12.12_spmd.clone, body=%wide.wide.region_11.11_spmd.clone.sunk | while | flops 135430720 | bytes 2039739 | solution.py:83
  258.7 44.9 %while.185 = (s32[]{:T(128)}, f32[512,128]{1,0:T(8,128)S(1)}, f32[8192,128]{1,0:T(8,128)}, f32[8192,128]{1,0:T(8,128)}, s32[]{:T(128)}, /*index=5*/s32[64]{0:T(1...) while((s32[]{:T(128)}, f32[512,128]{1,0:T(8,128)S(1)}, ...), condition=%wide.wide.region_15.15_spmd.clone, body=%wide.wide.region_14.14_spmd.clone.sunk | while | flops 337674816 | bytes 8332271 | solution.py:120
  308.9 18.7 %while.183 = (s32[]{:T(128)}, f32[64,8]{1,0:T(8,128)S(1)}, f32[64,8]{1,0:T(8,128)S(1)}, s32[]{:T(128)}, s32[64]{0:T(128)S(1)}, /*index=5*/bf16[8192,128]{1,0:T(8...) while((s32[]{:T(128)}, f32[64,8]{1,0:T(8,128)S(1)}, ...), condition=%wide.region_10.10_spmd.clone, body=%wide.region_7.9_spmd.clone.sunk | while | flops 68781640 | bytes 3779503 | solution.py:70
  328.3 17.5 %while.184 = (s32[]{:T(128)}, f32[512,128]{1,0:T(8,128)S(1)}, s32[]{:T(128)}, s32[64]{0:T(128)S(1)}, bf16[8192,128]{1,0:T(8,128)(2,1)}, /*index=5*/bf16[512,128]...) while((s32[]{:T(128)}, f32[512,128]{1,0:T(8,128)S(1)}, ...), condition=%wide.wide.region_12.12_spmd.clone, body=%wide.wide.region_11.11_spmd.clone.sunk | while | flops 135430720 | bytes 2039739 | solution.py:83
  346.7 53.9 %while.185 = (s32[]{:T(128)}, f32[512,128]{1,0:T(8,128)S(1)}, f32[8192,128]{1,0:T(8,128)}, f32[8192,128]{1,0:T(8,128)}, s32[]{:T(128)}, /*index=5*/s32[64]{0:T(1...) while((s32[]{:T(128)}, f32[512,128]{1,0:T(8,128)S(1)}, ...), condition=%wide.wide.region_15.15_spmd.clone, body=%wide.wide.region_14.14_spmd.clone.sunk | while | flops 337674816 | bytes 8332271 | solution.py:120
  405.9 3.1 while.183
  409.7 2.9 while.184
  413.5 9.0 while.185
  427.8 6.2 while.183
  434.7 5.8 while.184
  441.4 17.9 %while.185 = (s32[]{:T(128)}, f32[512,128]{1,0:T(8,128)S(1)}, f32[8192,128]{1,0:T(8,128)}, f32[8192,128]{1,0:T(8,128)}, s32[]{:T(128)}, /*index=5*/s32[64]{0:T(1...) while((s32[]{:T(128)}, f32[512,128]{1,0:T(8,128)S(1)}, ...), condition=%wide.wide.region_15.15_spmd.clone, body=%wide.wide.region_14.14_spmd.clone.sunk | while | flops 337674816 | bytes 8332271 | solution.py:120
  464.7 9.4 while.183
  474.7 8.7 while.184
  484.4 26.9 %while.185 = (s32[]{:T(128)}, f32[512,128]{1,0:T(8,128)S(1)}, f32[8192,128]{1,0:T(8,128)}, f32[8192,128]{1,0:T(8,128)}, s32[]{:T(128)}, /*index=5*/s32[64]{0:T(1...) while((s32[]{:T(128)}, f32[512,128]{1,0:T(8,128)S(1)}, ...), condition=%wide.wide.region_15.15_spmd.clone, body=%wide.wide.region_14.14_spmd.clone.sunk | while | flops 337674816 | bytes 8332271 | solution.py:120
  512.3 4.5 broadcast_multiply_fusion
  518.9 2.5 copy.80
  521.3 122.8 %all-to-all-start.2 = ((bf16[16,64,1024]{2,1,0:T(8,128)(2,1)}), bf16[16,64,1024]{2,1,0:T(8,128)(2,1)S(1)}, u32[]{:S(2)}, u32[]{:S(2)}) async-start(bf16[16,64,1024]{2,1,0:T(8,128)(2,1)} %copy.80), calls=%async_computation.2 | async-start | bytes 4194304 | tf_op jit(solution)/shard_map/all_to_all | solution.py:224
  644.1 2.1 convolution_convert_fusion
  646.2 2.5 copy.84
  648.7 24.2 %all-to-all-done.2 = bf16[16,64,1024]{2,1,0:T(8,128)(2,1)S(1)} async-done(((bf16[16,64,1024]{2,1,0:T(8,128)(2,1)}), bf16[16,64,1024]{2,1,0:T(8,128)(2,1)S(1)}, u32[]{:S(2)}, u32[]{:S(2)}) %all-to-all-start.2) | async-done | bytes 2097184 | tf_op jit(solution)/shard_map/all_to_all | solution.py:224
  672.9 5.1 all-to-all-start.3
  680.8 26.0 %all-to-all-done.3 = bf16[16,64,1024]{2,1,0:T(8,128)(2,1)} async-done(((bf16[16,64,1024]{2,1,0:T(8,128)(2,1)}), bf16[16,64,1024]{2,1,0:T(8,128)(2,1)}, u32[]{:S(2)}, u32[]{:S(2)}) %all-to-all-start.3) | async-done | bytes 2097184 | tf_op jit(solution)/shard_map/all_to_all | solution.py:225
  706.8 2.8 fusion.59
  711.2 148.1 %reduce-scatter.5.cloned.1.call-done = f32[512,128]{1,0:T(8,128)} async-done(((f32[8192,128]{1,0:T(8,128)}), f32[512,128]{1,0:T(8,128)}) %reduce-scatter.5.cloned.1.call-update) | async-done | bytes 262160 | tf_op jit(solution)/shard_map/reduce_scatter | solution.py:243
  860.9 91.4 %reduce-scatter.3.cloned.1.call-done = f32[512,128]{1,0:T(8,128)} async-done(((f32[8192,128]{1,0:T(8,128)}), f32[512,128]{1,0:T(8,128)}) %reduce-scatter.3.cloned.1.call-update) | async-done | bytes 262160 | tf_op jit(solution)/shard_map/reduce_scatter | solution.py:242
  (873 shorter events, 392.3 us)
Async XLA Ops:
  7.2 1.5 copy-start
  7.2 88.2 %all-gather.3.cloned.1.call-start = ((), (), s32[]{:S(2)}) async-start(), calls=%async_computation.6 | async-start | bytes 2228224 | tf_op jit(solution)/shard_map/all_gather | solution.py:203
  12.1 41.3 %all-to-all-start = ((bf16[16,64,1024]{2,1,0:T(8,128)(2,1)}), bf16[16,64,1024]{2,1,0:T(8,128)(2,1)S(1)}, u32[]{:S(2)}, u32[]{:S(2)}) async-start(bf16[16,64,1024]{2,1,0:T(8,128)(2,1)} %copy.72), calls=%async_computation | async-start | bytes 4194304 | tf_op jit(solution)/shard_map/all_to_all | solution.py:173
  17.6 87.5 %all-gather.5.cloned.1.call-start = ((), (), s32[]{:S(2)}) async-start(), calls=%async_computation.7 | async-start | bytes 2228224 | tf_op jit(solution)/shard_map/all_gather | solution.py:204
  23.0 35.1 %copy-start.3 = (s32[16]{0:T(128)S(1)}, s32[16]{0:T(128)}, u32[]{:S(2)}) copy-start(s32[16]{0:T(128)} %param.18) | copy-start | bytes 196
  23.0 35.7 %copy-start.4 = (s32[128]{0:T(128)S(1)}, s32[128]{0:T(128)}, u32[]{:S(2)}) copy-start(s32[128]{0:T(128)} %param.19) | copy-start | bytes 1540
  53.3 37.6 %all-to-all-start.1 = ((bf16[16,64,1024]{2,1,0:T(8,128)(2,1)}), bf16[16,64,1024]{2,1,0:T(8,128)(2,1)}, u32[]{:S(2)}, u32[]{:S(2)}) async-start(bf16[16,64,1024]{2,1,0:T(8,128)(2,1)} %copy.76), calls=%async_computation.1 | async-start | bytes 4194304 | tf_op jit(solution)/shard_map/all_to_all | solution.py:174
  57.8 801.5 %reduce-scatter.5.cloned.1.call-start = ((), (), s32[]{:S(2)}) async-start(), calls=%async_computation.9 | async-start | bytes 4456448 | tf_op jit(solution)/shard_map/reduce_scatter | solution.py:243
  119.5 0.6 copy-start.1
  144.5 0.6 copy-start.1
  184.5 0.6 copy-start.1
  242.6 0.6 copy-start.1
  327.7 0.6 copy-start.1
  409.0 0.6 copy-start.1
  434.1 0.6 copy-start.1
  474.1 0.6 copy-start.1
  512.0 440.3 %reduce-scatter.3.cloned.1.call-start = ((), (), s32[]{:S(2)}) async-start(), calls=%async_computation.8 | async-start | bytes 4456448 | tf_op jit(solution)/shard_map/reduce_scatter | solution.py:242
  516.8 1.2 copy-start.2
  521.3 151.5 %all-to-all-start.2 = ((bf16[16,64,1024]{2,1,0:T(8,128)(2,1)}), bf16[16,64,1024]{2,1,0:T(8,128)(2,1)S(1)}, u32[]{:S(2)}, u32[]{:S(2)}) async-start(bf16[16,64,1024]{2,1,0:T(8,128)(2,1)} %copy.80), calls=%async_computation.2 | async-start | bytes 4194304 | tf_op jit(solution)/shard_map/all_to_all | solution.py:224
  672.9 33.9 %all-to-all-start.3 = ((bf16[16,64,1024]{2,1,0:T(8,128)(2,1)}), bf16[16,64,1024]{2,1,0:T(8,128)(2,1)}, u32[]{:S(2)}, u32[]{:S(2)}) async-start(bf16[16,64,1024]{2,1,0:T(8,128)(2,1)} %copy.84), calls=%async_computation.3 | async-start | bytes 4194304 | tf_op jit(solution)/shard_map/all_to_all | solution.py:225
Sparse Core Ops, SparseCore 0:
  9.7 50.7 all-gather.2
  62.2 42.8 all-gather.4
  512.2 347.0 reduce-scatter.4
  861.5 90.7 reduce-scatter.2
where the time goes:
time: 970 us; the launch traced here: 960 us
  waiting for transfers between devices  359 us (37%)
  matrix products  258 us (27%)
  starting transfers between devices  138 us (14%)
  local copies, waits for them, and re-layouts  95.3 us (10%)
  other arithmetic  68 us (7%)
  loops' own time  27.8 us (3%)
  between operations  13.9 us (1%)
    reduce_scatter x1, waiting for transfers between devices, body(): lax.psum_scatter(value_term, 'context', scatter_dimension=0, tiled=True)  148 us
    all_to_all x1, starting transfers between devices, body(): lax.all_to_all(back_attn, 'context', split_axis=0, concat_axis=0, tiled=T...  123 us
    reduce_scatter x1, waiting for transfers between devices, body(): lax.psum_scatter(key_term, 'context', scatter_dimension=0, tiled=True)  91.4 us
    dot_general x46, matrix products, tile_scores(): lax.dot_general(query_tile, key_tile, (((1,), (1,)), ((), ())), preferred...  58.8 us
    dot_general x23, matrix products, grad_pass(): lax.dot_general(weights_low, grad_tile, (((0,), (0,)), ((), ())), preferr...  45.2 us
    dot_general x23, matrix products, grad_pass(): lax.dot_general(grad_scores, query_tile, (((0,), (0,)), ((), ())), prefer...  44.8 us
    add x69, other arithmetic, one_block(): row_pos = first + jnp.arange(block_rows, dtype=jnp.int32)  43.7 us
    dot_general x23, matrix products, output_pass(): jnp.dot(weights_low, value_tile, preferred_element_type=jnp.float32)  37.8 us
  transfers between devices with their start and end apart: 8, of which 7 were waited for; matrix products, arithmetic and copies ran while one was open for 4% of the time, Pallas kernels for 0%

commit v1 on v0

v1 whole, which is shorter than its diff:
```python
import functools
import math

import jax
import jax.numpy as jnp
from jax import lax
from jax.experimental import pallas as pl
from jax.experimental.pallas import tpu as pltpu
from jax.sharding import PartitionSpec as P

NEG_FILL = -1e30
MESH = pl.DeviceIdType.MESH
YS = 4
HD = 128
GROUP = 4
TILE = 256
SPAN = 4
PASS = 512
ONES = 16
LARGE = 1e12
QBLOCK = 256
DOC_MAX = 4096


def place():
    me = lax.axis_index("context")
    return me // (2 * YS), (me // 2) % YS, me % 2


def rank_of(x, y, core):
    return (x * YS + y) * 2 + core


def remote(src, dst, send_sem, recv_sem, rank):
    return pltpu.make_async_remote_copy(
        src_ref=src,
        dst_ref=dst,
        send_sem=send_sem,
        recv_sem=recv_sem,
        device_id={"context": rank},
        device_id_type=MESH,
    )


def enter(x, y, core):
    barrier = pltpu.get_barrier_semaphore()
    others = [
        rank_of(x, y, 1 - core),
        rank_of(1 - x, y, core),
        rank_of(1 - x, y, 1 - core),
        rank_of(x, (y + 1) % YS, core),
        rank_of(x, (y + YS - 1) % YS, core),
    ]
    for other in others:
        pl.semaphore_signal(barrier, inc=1, device_id={"context": other}, device_id_type=MESH)
    pl.semaphore_wait(barrier, len(others))


def rows_at(begin, count):
    return pl.ds(pl.multiple_of(begin, count), count)


def gather_kernel(
    q_ref, g_ref, k_ref, v_ref, qa_ref, ga_ref, ka_ref, va_ref,
    own_sem, kv_send, kv_recv, core_send, core_recv, row_send, row_recv,
):
    x, y, core = place()
    shard = k_ref.shape[0]
    half = shard // 2
    width = qa_ref.shape[1]
    up, down, far = (y + 1) % YS, (y + YS - 1) % YS, (y + 2) % YS
    slot = x * 2 + core
    x_rank = rank_of(1 - x, y, core)
    core_rank = rank_of(x, y, 1 - core)
    up_rank, down_rank = rank_of(x, up, core), rank_of(x, down, core)
    enter(x, y, core)
    started = []

    def send(src, dst, send_sem, recv_sem, rank):
        copy = remote(src, dst, send_sem, recv_sem, rank)
        copy.start()
        started.append(copy)

    def landed(ref, recv_sem):
        remote(ref, ref, recv_sem, recv_sem, x_rank).wait_recv()

    own = []
    pairs = ((k_ref, ka_ref), (v_ref, va_ref))
    my_rows = rows_at(rank_of(x, y, core) * shard, shard)
    for a, (src, dst) in enumerate(pairs):
        send(src, dst.at[my_rows], kv_send.at[a, 0], kv_recv.at[a, 0], x_rank)
        send(src, dst.at[my_rows], kv_send.at[a, 1], kv_recv.at[a, 1], up_rank)
        send(src, dst.at[my_rows], kv_send.at[a, 2], kv_recv.at[a, 2], down_rank)
        send(src, dst.at[my_rows], core_send.at[a, 0], core_recv.at[a, 0], core_rank)
        copy = pltpu.make_async_copy(src, dst.at[my_rows], own_sem.at[a])
        copy.start()
        own.append(copy)

    def head_cols(owner):
        return pl.ds(pl.multiple_of(owner * width, width), width)

    for a, (src, dst) in enumerate(((q_ref, qa_ref), (g_ref, ga_ref))):
        copy = pltpu.make_async_copy(
            src.at[:, head_cols(slot)], dst.at[rows_at(slot * shard, shard)], own_sem.at[2 + a]
        )
        copy.start()
        own.append(copy)
        for d, (dx, dc) in enumerate(((0, 1), (1, 0), (1, 1))):
            tx, tc = (x + dx) % 2, (core + dc) % 2
            send(
                src.at[:, head_cols(tx * 2 + tc)],
                dst.at[rows_at(slot * shard, shard)],
                row_send.at[a, d],
                row_recv.at[a, d],
                rank_of(tx, y, tc),
            )

    def forward(a, n, ref, rows, rank, relay):
        send(ref.at[rows], ref.at[rows], relay[0].at[a, n], relay[1].at[a, n], rank)

    y_relay, c_relay = (kv_send, kv_recv), (core_send, core_recv)

    def shard_rows(sx, sy, sc):
        return rows_at(rank_of(sx, sy, sc) * shard, shard)

    def half_rows(sx, sy, sc, h):
        return rows_at(rank_of(sx, sy, sc) * shard + h * half, half)

    for a, (_, dst) in enumerate(pairs):
        rows = shard_rows(1 - x, y, core)
        landed(dst.at[rows], kv_recv.at[a, 0])
        forward(a, 3, dst, rows, up_rank, y_relay)
        forward(a, 4, dst, rows, down_rank, y_relay)
        forward(a, 1, dst, rows, core_rank, c_relay)
    for n, sx in ((1, x), (3, 1 - x)):
        for a, (_, dst) in enumerate(pairs):
            landed(dst.at[shard_rows(sx, down, core)], kv_recv.at[a, n])
            forward(a, 4 + n, dst, half_rows(sx, down, core, 0), up_rank, y_relay)
            landed(dst.at[shard_rows(sx, up, core)], kv_recv.at[a, n + 1])
            forward(a, 5 + n, dst, half_rows(sx, up, core, 1), down_rank, y_relay)
            forward(a, 1 + n, dst, shard_rows(sx, down, core), core_rank, c_relay)
            forward(a, 2 + n, dst, shard_rows(sx, up, core), core_rank, c_relay)
    for n, sx in ((1, x), (3, 1 - x)):
        for a, (_, dst) in enumerate(pairs):
            for h in range(2):
                rows = half_rows(sx, far, core, h)
                landed(dst.at[rows], kv_recv.at[a, 4 + n + h])
                forward(a, 5 + n + h, dst, rows, core_rank, c_relay)
    for a, (_, dst) in enumerate(pairs):
        oc = 1 - core
        whole = ((x, y), (1 - x, y), (x, down), (x, up), (1 - x, down), (1 - x, up))
        for n, (sx, sy) in enumerate(whole):
            landed(dst.at[shard_rows(sx, sy, oc)], core_recv.at[a, n])
        for n, sx in ((1, x), (3, 1 - x)):
            for h in range(2):
                landed(dst.at[half_rows(sx, far, oc, h)], core_recv.at[a, 5 + n + h])
    for a, dst in enumerate((qa_ref, ga_ref)):
        for d, (dx, dc) in enumerate(((0, 1), (1, 0), (1, 1))):
            tx, tc = (x + dx) % 2, (core + dc) % 2
            landed(dst.at[rows_at((tx * 2 + tc) * shard, shard)], row_recv.at[a, d])
    for copy in own:
        copy.wait()
    for copy in started:
        copy.wait_send()


def gather(queries, out_grad, keys, values, ranks):
    shard, feature = queries.shape
    width = feature // GROUP
    bf16 = jnp.bfloat16
    any_spec = pl.BlockSpec(memory_space=pl.ANY)
    dma = pltpu.SemaphoreType.DMA
    return pl.pallas_call(
        gather_kernel,
        in_specs=[any_spec] * 4,
        out_specs=[any_spec] * 4,
        out_shape=[
            jax.ShapeDtypeStruct((GROUP * shard, width), bf16),
            jax.ShapeDtypeStruct((GROUP * shard, width), bf16),
            jax.ShapeDtypeStruct((ranks * shard, HD), bf16),
            jax.ShapeDtypeStruct((ranks * shard, HD), bf16),
        ],
        scratch_shapes=[
            dma((4,)), dma((2, 9)), dma((2, 9)), dma((2, 10)), dma((2, 10)), dma((2, 3)), dma((2, 3)),
        ],
        compiler_params=pltpu.CompilerParams(collective_id=0, has_side_effects=True),
        name="gather",
    )(queries, out_grad, keys, values)


def dot(a, b):
    return jnp.dot(a, b, preferred_element_type=jnp.float32)


def attend_kernel(
    len_ref, owner_ref, q_ref, g_ref, k_ref, v_ref, o_ref, dq_ref, dk_ref, dv_ref, pair_ref,
    kt_ref, vt_ref, p_ref, qt_ref, gt_ref, qn_ref, gn_ref, dka_ref, dva_ref, ds_ref, acc_ref,
):
    blk = pl.program_id(0)
    block, width = q_ref.shape
    heads = width // HD
    cols = block * heads
    tokens = k_ref.shape[0]
    docs = len_ref.shape[0]
    f32, bf16 = jnp.float32, jnp.bfloat16
    scale = 1.0 / math.sqrt(HD)
    scale2 = scale * math.log2(math.e)
    _, y, _ = place()
    per_chip = tokens // (2 * YS)
    per_range = pl.num_programs(0) // 2

    @pl.when(blk == 0)
    def _():
        def prepare(i, carry):
            rows = rows_at(i * PASS, PASS)
            kt_ref[:, rows] = k_ref[rows, :].T
            vt_ref[0:HD, rows] = v_ref[rows, :].T
            vt_ref[HD:, rows] = jnp.ones((ONES, PASS), bf16)
            dka_ref[rows, :] = jnp.zeros((PASS, HD), f32)
            dva_ref[rows, :] = jnp.zeros((PASS, HD), f32)
            return carry

        lax.fori_loop(0, tokens // PASS, prepare, 0)
        blocks = owner_ref.shape[1]
        block_rows = tokens // blocks
        shape = (block_rows, blocks)
        pos = lax.broadcasted_iota(jnp.int32, shape, 1) * block_rows
        pos = pos + lax.broadcasted_iota(jnp.int32, shape, 0)
        begin, end = jnp.zeros(shape, jnp.int32), jnp.int32(0)
        for d in range(docs):
            end = end + len_ref[d]
            begin = jnp.where(pos >= end, end, begin)
        counts = (pos - begin + 1).astype(f32)
        counts = jnp.where(owner_ref[...] == lax.axis_index("context"), counts, 0.0)
        pair_ref[0] = jnp.sum(counts)

    first = (blk // per_range) * (tokens // 2) + y * per_chip + lax.rem(blk, per_range) * block
    row_pos = first + lax.rem(lax.broadcasted_iota(jnp.int32, (1, cols), 1), block)
    row_start = jnp.zeros((1, cols), jnp.int32)
    first_start, last_start, end = jnp.int32(0), jnp.int32(0), jnp.int32(0)
    for d in range(docs):
        end = end + len_ref[d]
        row_start = jnp.where(row_pos >= end, end, row_start)
        first_start = jnp.where(first >= end, end, first_start)
        last_start = jnp.where(first + block - 1 >= end, end, last_start)
    low = lax.div(first_start, TILE)
    high = lax.div(first + block - 1, TILE) + 1

    own_keys = kt_ref[:, rows_at(first, block)].astype(f32)
    shift = []
    for h in range(heads):
        q_t = q_ref[:, h * HD : (h + 1) * HD].T
        qt_ref[:, h * block : (h + 1) * block] = q_t
        gt_ref[:, h * block : (h + 1) * block] = g_ref[:, h * HD : (h + 1) * HD].T
        shift.append(jnp.sum(q_t.astype(f32) * own_keys, axis=0, keepdims=True) * scale2)
    shift = jnp.concatenate(shift, axis=1)

    def key_rows(t, count):
        return pl.ds(pl.multiple_of(t * TILE, TILE), count)

    def kept_rows(t, count):
        return pl.ds(pl.multiple_of((t - low) * TILE, TILE), count)

    def sweep(piece):
        count = high - low
        groups = lax.div(count, SPAN)

        def one(g, carry):
            piece(low + g * SPAN, SPAN * TILE, False)
            return carry

        lax.fori_loop(0, groups, one, 0)
        at = low + groups * SPAN
        size = SPAN // 2
        while size:
            has = lax.rem(lax.div(count, size), 2)

            @pl.when(has == 1)
            def _(at=at, size=size):
                piece(at, size * TILE, True)

            at = at + has * size
            size //= 2

    def forward(shift):
        acc_ref[...] = jnp.zeros(acc_ref.shape, f32)

        def piece(t, rows, last):
            def run(mask):
                acc = None
                part = min(rows, PASS)
                for i in range(0, rows, part):
                    tile = t + i // TILE
                    s = dot(k_ref[key_rows(tile, part), :], qt_ref[...]) * scale2 - shift
                    if mask:
                        pos = t * TILE + i + lax.broadcasted_iota(jnp.int32, s.shape, 0)
                        s = jnp.where((pos >= row_start) & (pos <= row_pos), s, NEG_FILL)
                    p_ref[kept_rows(tile, part), :] = jnp.exp2(s).astype(bf16)
                    term = dot(vt_ref[:, key_rows(tile, part)], p_ref[kept_rows(tile, part), :])
                    acc = term if acc is None else acc + term
                acc_ref[...] += acc

            if last:
                run(True)
            else:
                edge = (t * TILE < last_start) | (t * TILE + rows - 1 > first)
                pl.when(edge)(lambda: run(True))
                pl.when(jnp.logical_not(edge))(lambda: run(False))

        sweep(piece)

    forward(shift)

    @pl.when(jnp.logical_not(jnp.max(acc_ref[HD : HD + 1, :]) < LARGE))
    def _():
        def peak_pass(t, peak):
            s = dot(k_ref[key_rows(t, TILE), :], qt_ref[...]) * scale2
            pos = t * TILE + lax.broadcasted_iota(jnp.int32, s.shape, 0)
            s = jnp.where((pos >= row_start) & (pos <= row_pos), s, NEG_FILL)
            return jnp.maximum(peak, jnp.max(s.reshape(TILE // 8, 8, cols), axis=0))

        peak = lax.fori_loop(low, high, peak_pass, jnp.full((8, cols), NEG_FILL, f32))
        forward(jnp.max(peak, axis=0, keepdims=True))

    inverse = 1.0 / acc_ref[HD : HD + 1, :]
    out = (acc_ref[0:HD, :] * inverse).astype(bf16)
    grad_t = gt_ref[...].astype(f32)
    grad_dot = jnp.sum(out.astype(f32) * grad_t, axis=0, keepdims=True)
    gn_ref[...] = (grad_t * inverse).astype(bf16).T
    qn_ref[...] = (qt_ref[...].astype(f32) * inverse).astype(bf16).T
    out = out.T
    for h in range(heads):
        o_ref[:, h * HD : (h + 1) * HD] = out[h * block : (h + 1) * block, :]
    acc_ref[0:HD, :] = jnp.zeros((HD, cols), f32)

    def backward(t, rows, last):
        keys, kept = key_rows(t, rows), kept_rows(t, rows)
        grad_p = dot(v_ref[keys, :], gt_ref[...])
        ds_ref[0:rows, :] = (p_ref[kept, :].astype(f32) * (grad_p - grad_dot)).astype(bf16)
        dva_ref[keys, :] += dot(p_ref[kept, :], gn_ref[...])
        dka_ref[keys, :] += dot(ds_ref[0:rows, :], qn_ref[...])
        acc_ref[0:HD, :] += dot(kt_ref[:, keys], ds_ref[0:rows, :])

    sweep(backward)
    query_grad = (acc_ref[0:HD, :] * (inverse * scale)).astype(bf16).T
    for h in range(heads):
        dq_ref[:, h * HD : (h + 1) * HD] = query_grad[h * block : (h + 1) * block, :]

    @pl.when(blk == pl.num_programs(0) - 1)
    def _():
        def finish(i, carry):
            rows = rows_at(i * PASS, PASS)
            dk_ref[rows, :] = (dka_ref[rows, :] * scale).astype(bf16)
            dv_ref[rows, :] = dva_ref[rows, :].astype(bf16)
            return carry

        lax.fori_loop(0, tokens // PASS, finish, 0)


def attend(queries, out_grad, keys, values, lengths, block_owner):
    rows, width = queries.shape
    tokens = keys.shape[0]
    cols = QBLOCK * (width // HD)
    span = ((DOC_MAX + QBLOCK + TILE - 2) // TILE + 1) * TILE
    row_spec = pl.BlockSpec((QBLOCK, width), lambda i, *_: (i, 0))
    full_spec = pl.BlockSpec((tokens, HD), lambda i, *_: (0, 0))
    owner_spec = pl.BlockSpec((1, block_owner.shape[0]), lambda i, *_: (0, 0))
    bf16, f32 = jnp.bfloat16, jnp.float32
    return pl.pallas_call(
        attend_kernel,
        grid_spec=pltpu.PrefetchScalarGridSpec(
            num_scalar_prefetch=1,
            grid=(rows // QBLOCK,),
            in_specs=[owner_spec, row_spec, row_spec, full_spec, full_spec],
            out_specs=[
                row_spec, row_spec, full_spec, full_spec, pl.BlockSpec(memory_space=pltpu.SMEM),
            ],
            scratch_shapes=[
                pltpu.VMEM((HD, tokens), bf16),
                pltpu.VMEM((HD + ONES, tokens), bf16),
                pltpu.VMEM((span, cols), bf16),
                pltpu.VMEM((HD, cols), bf16),
                pltpu.VMEM((HD, cols), bf16),
                pltpu.VMEM((cols, HD), bf16),
                pltpu.VMEM((cols, HD), bf16),
                pltpu.VMEM((tokens, HD), f32),
                pltpu.VMEM((tokens, HD), f32),
                pltpu.VMEM((SPAN * TILE, cols), bf16),
                pltpu.VMEM((HD + ONES, cols), f32),
            ],
        ),
        out_shape=[
            jax.ShapeDtypeStruct((rows, width), bf16),
            jax.ShapeDtypeStruct((rows, width), bf16),
            jax.ShapeDtypeStruct((tokens, HD), bf16),
            jax.ShapeDtypeStruct((tokens, HD), bf16),
            jax.ShapeDtypeStruct((1,), f32),
        ],
        compiler_params=pltpu.CompilerParams(vmem_limit_bytes=62 * 2**20),
        name="attend",
    )(lengths, block_owner.reshape(1, -1), queries, out_grad, keys, values)


def scatter_kernel(
    oa_ref, qa_ref, dk_ref, dv_ref, o_ref, q_ref, key_ref, value_ref,
    part, from_core, from_far, from_near, from_x,
    own_sem, part_sem, core_send, core_recv, far_send, far_recv, near_send, near_recv,
    x_send, x_recv, row_send, row_recv,
):
    x, y, core = place()
    shard = key_ref.shape[0]
    half = shard // 2
    width = oa_ref.shape[1]
    up, down, far = (y + 1) % YS, (y + YS - 1) % YS, (y + 2) % YS
    slot = x * 2 + core
    x_rank = rank_of(1 - x, y, core)
    core_rank = rank_of(x, y, 1 - core)
    up_rank, down_rank = rank_of(x, up, core), rank_of(x, down, core)
    started, own = [], []

    def send(src, dst, send_sem, recv_sem, rank):
        copy = remote(src, dst, send_sem, recv_sem, rank)
        copy.start()
        started.append(copy)

    def landed(ref, recv_sem):
        remote(ref, ref, recv_sem, recv_sem, x_rank).wait_recv()

    pairs = (dk_ref, dv_ref)
    order = [(1 - x, far), (x, far), (1 - x, up), (x, up), (1 - x, down), (x, down), (1 - x, y), (x, y)]
    loads = []
    for n, (sx, sy) in enumerate(order):
        for a, src in enumerate(pairs):
            rows = rows_at(rank_of(sx, sy, core) * shard, shard)
            copy = pltpu.make_async_copy(src.at[rows], part.at[a, n], part_sem.at[a, n])
            copy.start()
            loads.append(copy)
    enter(x, y, core)
    for n, (sx, sy) in enumerate(order):
        for a, src in enumerate(pairs):
            rows = rows_at(rank_of(sx, sy, 1 - core) * shard, shard)
            send(src.at[rows], from_core.at[a, n], core_send.at[a, n], core_recv.at[a, n], core_rank)

    def head_cols(owner):
        return pl.ds(pl.multiple_of(owner * width, width), width)

    for a, (src, dst) in enumerate(((oa_ref, o_ref), (qa_ref, q_ref))):
        copy = pltpu.make_async_copy(
            src.at[rows_at(slot * shard, shard)], dst.at[:, head_cols(slot)], own_sem.at[a]
        )
        copy.start()
        own.append(copy)
        for d, (dx, dc) in enumerate(((0, 1), (1, 0), (1, 1))):
            tx, tc = (x + dx) % 2, (core + dc) % 2
            send(
                src.at[rows_at((tx * 2 + tc) * shard, shard)],
                dst.at[:, head_cols(slot)],
                row_send.at[a, d],
                row_recv.at[a, d],
                rank_of(tx, y, tc),
            )

    def add(ref, other):
        ref[...] = (ref[...].astype(jnp.float32) + other[...].astype(jnp.float32)).astype(jnp.bfloat16)

    def core_sum(a, n):
        loads[2 * n + a].wait()
        landed(from_core.at[a, n], core_recv.at[a, n])
        add(part.at[a, n], from_core.at[a, n])

    for n in range(2):
        for a in range(2):
            core_sum(a, n)
            for h, rank in ((0, up_rank), (1, down_rank)):
                send(
                    part.at[a, n, pl.ds(h * half, half)], from_far.at[a, n, h],
                    far_send.at[a, n, h], far_recv.at[a, n, h], rank,
                )
    for n in range(2):
        for a in range(2):
            for j, rank in ((0, up_rank), (1, down_rank)):
                core_sum(a, 2 + 2 * j + n)
                free = 1 - j
                send(
                    part.at[a, 2 + 2 * j + n, pl.ds(free * half, half)],
                    from_near.at[a, n, j, pl.ds(free * half, half)],
                    near_send.at[a, n, j, free], near_recv.at[a, n, j, free], rank,
                )
    for n in range(2):
        for a in range(2):
            for j, rank in ((0, up_rank), (1, down_rank)):
                landed(from_far.at[a, n, j], far_recv.at[a, n, j])
                mine = part.at[a, 2 + 2 * j + n, pl.ds(j * half, half)]
                add(mine, from_far.at[a, n, j])
                send(
                    mine, from_near.at[a, n, j, pl.ds(j * half, half)],
                    near_send.at[a, n, j, j], near_recv.at[a, n, j, j], rank,
                )
    for n in range(2):
        for a in range(2):
            core_sum(a, 6 + n)
            for j in range(2):
                for h in (1 - j, j):
                    landed(from_near.at[a, n, j, pl.ds(h * half, half)], near_recv.at[a, n, j, h])
            total = part[a, 6 + n].astype(jnp.float32)
            total = total + from_near[a, n, 0].astype(jnp.float32)
            total = total + from_near[a, n, 1].astype(jnp.float32)
            part[a, 6 + n] = total.astype(jnp.bfloat16)
            if n == 0:
                send(part.at[a, 6], from_x.at[a], x_send.at[a], x_recv.at[a], x_rank)
    for a, dst in enumerate((key_ref, value_ref)):
        landed(from_x.at[a], x_recv.at[a])
        dst[...] = (part[a, 7].astype(jnp.float32) + from_x[a].astype(jnp.float32)).astype(jnp.bfloat16)
    for a, dst in enumerate((o_ref, q_ref)):
        for d, (dx, dc) in enumerate(((0, 1), (1, 0), (1, 1))):
            tx, tc = (x + dx) % 2, (core + dc) % 2
            landed(dst.at[:, head_cols(tx * 2 + tc)], row_recv.at[a, d])
    for copy in own:
        copy.wait()
    for copy in started:
        copy.wait_send()


def scatter(out_rows, query_rows, key_terms, value_terms, ranks):
    rows, width = out_rows.shape
    shard = rows // GROUP
    half = shard // 2
    bf16 = jnp.bfloat16
    any_spec = pl.BlockSpec(memory_space=pl.ANY)
    vmem_spec = pl.BlockSpec(memory_space=pltpu.VMEM)
    dma = pltpu.SemaphoreType.DMA
    return pl.pallas_call(
        scatter_kernel,
        in_specs=[any_spec] * 4,
        out_specs=[any_spec, any_spec, vmem_spec, vmem_spec],
        out_shape=[
            jax.ShapeDtypeStruct((shard, width * GROUP), bf16),
            jax.ShapeDtypeStruct((shard, width * GROUP), bf16),
            jax.ShapeDtypeStruct((shard, HD), bf16),
            jax.ShapeDtypeStruct((shard, HD), bf16),
        ],
        scratch_shapes=[
            pltpu.VMEM((2, ranks // 2, shard, HD), bf16),
            pltpu.VMEM((2, ranks // 2, shard, HD), bf16),
            pltpu.VMEM((2, 2, 2, half, HD), bf16),
            pltpu.VMEM((2, 2, 2, shard, HD), bf16),
            pltpu.VMEM((2, shard, HD), bf16),
            dma((2,)), dma((2, 8)), dma((2, 8)), dma((2, 8)), dma((2, 2, 2)), dma((2, 2, 2)),
            dma((2, 2, 2, 2)), dma((2, 2, 2, 2)), dma((2,)), dma((2,)), dma((2, 3)), dma((2, 3)),
        ],
        compiler_params=pltpu.CompilerParams(
            collective_id=1, has_side_effects=True, vmem_limit_bytes=40 * 2**20
        ),
        name="scatter",
    )(out_rows, query_rows, key_terms, value_terms)


def body(queries, key_rows, values, out_grad, lengths, block_owner):
    ranks = lax.axis_size("context")
    queries, out_grad, keys, values = gather(queries, out_grad, key_rows, values, ranks)
    out, query_grad, key_terms, value_terms, pair_count = attend(
        queries, out_grad, keys, values, lengths, block_owner
    )
    out, query_grad, key_grad, value_grad = scatter(out, query_grad, key_terms, value_terms, ranks)
    return out, query_grad, key_grad, value_grad, pair_count


def solution(mesh):
    rows = P(("dp", "context"), None)
    return jax.shard_map(
        body,
        mesh=mesh,
        in_specs=(rows, rows, rows, rows, P("dp"), P("dp")),
        out_specs=(rows, rows, rows, rows, P(("dp", "context"))),
        check_vma=False,
    )
```

time: 970 us -> 137 us (0.14)
  the two profiles are of different devices: /device:TPU:96 before, /device:TPU:64 now
where the time goes in v1:
time: 137 us
  Pallas kernels  127 us (93%)
  local copies, waits for them, and re-layouts  8.87 us (6%)
    pallas_call x1, Pallas kernels, attend(): pl.pallas_call(attend_kernel, grid_spec=pltpu.PrefetchScalarGridSpec(num_...  57.2 us
    pallas_call x1, Pallas kernels, scatter(): pl.pallas_call(scatter_kernel, in_specs=[any_spec] * 4, out_specs=[any_sp...  36.7 us
    pallas_call x1, Pallas kernels, gather(): pl.pallas_call(gather_kernel, in_specs=[any_spec] * 4, out_specs=[any_spe...  33.2 us
    unnamed x12, local copies, waits for them, and re-layouts  8.87 us

profile of v1, /device:TPU:64, one launch (start us, length us, event | category | flops | bytes accessed | tf_op | source)
XLA Modules:
  0.0 136.7 jit_solution(13658530665574135215)
XLA Ops:
  0.6 33.2 %gather.1 = (bf16[2048,256]{1,0:T(8,128)(2,1)}, bf16[2048,256]{1,0:T(8,128)(2,1)}, bf16[8192,128]{1,0:T(8,128)(2,1)}, bf16[8192,128]{1,0:T(8,128)(2,1)}) custom-call(bf16[512,1024]{1,0:T(8,128)(2,1)} %q_ref.1, bf16[512,1024]{1,0:T(8,128)(2,1)} %g_ref.1, bf16[512,128]{1,0:T(8,128)(2,1)} %k_ref.1, bf16[512,128]{1,0:T(8,128)(2,1)} %v_ref.1), custom_call_target="tpu_custom_call" | custom-call | tf_op jit(solution)/shard_map/gather/pallas_call | solution.py:173
  33.8 57.2 %attend.1 = (bf16[2048,256]{1,0:T(8,128)(2,1)}, bf16[2048,256]{1,0:T(8,128)(2,1)}, bf16[8192,128]{1,0:T(8,128)(2,1)}, bf16[8192,128]{1,0:T(8,128)(2,1)}, f32[1]{0:T(128)}) custom-call(s32[16]{0:T(128)} %len_ref.1, s32[1,128]{1,0:T(1,128)} %bitcast.1, bf16[2048,256]{1,0:T(8,128)(2,1)} %get-tuple-element.18.q_ref, bf16[2048,256]{1,0:T(8,128)(2,1)} %get-tuple-element.19.g_ref, ...), custom_call_target="tpu_custom_call" | custom-call | tf_op jit(solution)/shard_map/attend/pallas_call | solution.py:369
  91.1 0.0 copy-start
  91.1 1.6 %copy-done = bf16[8192,128]{1,0:T(8,128)(2,1)S(1)} copy-done((bf16[8192,128]{1,0:T(8,128)(2,1)S(1)}, bf16[8192,128]{1,0:T(8,128)(2,1)}, u32[]{:S(2)}) %copy-start) | copy-done | bytes 2097176
  92.7 0.0 copy-start.1
  92.7 1.6 %copy-done.1 = bf16[8192,128]{1,0:T(8,128)(2,1)S(1)} copy-done((bf16[8192,128]{1,0:T(8,128)(2,1)S(1)}, bf16[8192,128]{1,0:T(8,128)(2,1)}, u32[]{:S(2)}) %copy-start.1) | copy-done | bytes 2097176
  94.3 0.0 copy-start.2
  94.3 1.2 copy-done.2
  95.5 0.0 copy-start.3
  95.5 1.2 copy-done.3
  96.7 36.7 %scatter.1 = (bf16[512,1024]{1,0:T(8,128)(2,1)S(1)}, bf16[512,1024]{1,0:T(8,128)(2,1)S(1)}, bf16[512,128]{1,0:T(8,128)(2,1)S(1)}, bf16[512,128]{1,0:T(8,128)(2,1)S(1)}) custom-call(bf16[2048,256]{1,0:T(8,128)(2,1)S(1)} %copy-done.2, bf16[2048,256]{1,0:T(8,128)(2,1)S(1)} %copy-done.3, bf16[8192,128]{1,0:T(8,128)(2,1)S(1)} %copy-done, ...), custom_call_target="tpu_custom_call" | custom-call | tf_op jit(solution)/shard_map/scatter/pallas_call | solution.py:532
  133.4 1.0 copy.15
  134.4 1.0 copy.16
  135.4 0.7 copy.17
  136.0 0.7 copy.18
Async XLA Ops:
  91.1 1.6 %copy-start = (bf16[8192,128]{1,0:T(8,128)(2,1)S(1)}, bf16[8192,128]{1,0:T(8,128)(2,1)}, u32[]{:S(2)}) copy-start(bf16[8192,128]{1,0:T(8,128)(2,1)} %get-tuple-element.24.dk_ref) | copy-start | bytes 6291460
  92.7 1.6 %copy-start.1 = (bf16[8192,128]{1,0:T(8,128)(2,1)S(1)}, bf16[8192,128]{1,0:T(8,128)(2,1)}, u32[]{:S(2)}) copy-start(bf16[8192,128]{1,0:T(8,128)(2,1)} %get-tuple-element.25.dv_ref) | copy-start | bytes 6291460
  94.3 1.2 copy-start.2
  95.5 1.2 copy-start.3

commit v2 on v1

--- a/solution.py
+++ b/solution.py
@@ -12,6 +12,7 @@
 MESH = pl.DeviceIdType.MESH
 YS = 4
 HD = 128
+HEADS_HERE = 2
 GROUP = 4
 TILE = 256
 SPAN = 4
@@ -47,7 +48,6 @@
     others = [
         rank_of(x, y, 1 - core),
         rank_of(1 - x, y, core),
-        rank_of(1 - x, y, 1 - core),
         rank_of(x, (y + 1) % YS, core),
         rank_of(x, (y + YS - 1) % YS, core),
     ]
@@ -61,15 +61,14 @@
 
 
 def gather_kernel(
-    q_ref, g_ref, k_ref, v_ref, qa_ref, ga_ref, ka_ref, va_ref,
+    q_ref, g_ref, k_ref, v_ref, rows_ref, ka_ref, va_ref,
     own_sem, kv_send, kv_recv, core_send, core_recv, row_send, row_recv,
 ):
     x, y, core = place()
     shard = k_ref.shape[0]
     half = shard // 2
-    width = qa_ref.shape[1]
+    width = q_ref.shape[1] // GROUP
     up, down, far = (y + 1) % YS, (y + YS - 1) % YS, (y + 2) % YS
-    slot = x * 2 + core
     x_rank = rank_of(1 - x, y, core)
     core_rank = rank_of(x, y, 1 - core)
     up_rank, down_rank = rank_of(x, up, core), rank_of(x, down, core)
@@ -96,24 +95,12 @@
         copy.start()
         own.append(copy)
 
-    def head_cols(owner):
-        return pl.ds(pl.multiple_of(owner * width, width), width)
-
-    for a, (src, dst) in enumerate(((q_ref, qa_ref), (g_ref, ga_ref))):
-        copy = pltpu.make_async_copy(
-            src.at[:, head_cols(slot)], dst.at[rows_at(slot * shard, shard)], own_sem.at[2 + a]
+    for a, src in enumerate((q_ref, g_ref)):
+        cols = pl.ds(pl.multiple_of((x * 2 + 1 - core) * width, width), width)
+        send(
+            src.at[:, cols], rows_ref.at[:, pl.ds(a * width, width)],
+            row_send.at[a], row_recv.at[a], core_rank,
         )
-        copy.start()
-        own.append(copy)
-        for d, (dx, dc) in enumerate(((0, 1), (1, 0), (1, 1))):
-            tx, tc = (x + dx) % 2, (core + dc) % 2
-            send(
-                src.at[:, head_cols(tx * 2 + tc)],
-                dst.at[rows_at(slot * shard, shard)],
-                row_send.at[a, d],
-                row_recv.at[a, d],
-                rank_of(tx, y, tc),
-            )
 
     def forward(a, n, ref, rows, rank, relay):
         send(ref.at[rows], ref.at[rows], relay[0].at[a, n], relay[1].at[a, n], rank)
@@ -154,10 +141,8 @@
         for n, sx in ((1, x), (3, 1 - x)):
             for h in range(2):
                 landed(dst.at[half_rows(sx, far, oc, h)], core_recv.at[a, 5 + n + h])
-    for a, dst in enumerate((qa_ref, ga_ref)):
-        for d, (dx, dc) in enumerate(((0, 1), (1, 0), (1, 1))):
-            tx, tc = (x + dx) % 2, (core + dc) % 2
-            landed(dst.at[rows_at((tx * 2 + tc) * shard, shard)], row_recv.at[a, d])
+    for a in range(2):
+        landed(rows_ref.at[:, pl.ds(a * width, width)], row_recv.at[a])
     for copy in own:
         copy.wait()
     for copy in started:
@@ -173,17 +158,16 @@
     return pl.pallas_call(
         gather_kernel,
         in_specs=[any_spec] * 4,
-        out_specs=[any_spec] * 4,
+        out_specs=[any_spec] * 3,
         out_shape=[
-            jax.ShapeDtypeStruct((GROUP * shard, width), bf16),
-            jax.ShapeDtypeStruct((GROUP * shard, width), bf16),
+            jax.ShapeDtypeStruct((shard, 2 * width), bf16),
             jax.ShapeDtypeStruct((ranks * shard, HD), bf16),
             jax.ShapeDtypeStruct((ranks * shard, HD), bf16),
         ],
         scratch_shapes=[
-            dma((4,)), dma((2, 9)), dma((2, 9)), dma((2, 10)), dma((2, 10)), dma((2, 3)), dma((2, 3)),
+            dma((2,)), dma((2, 9)), dma((2, 9)), dma((2, 10)), dma((2, 10)), dma((2,)), dma((2,)),
         ],
-        compiler_params=pltpu.CompilerParams(collective_id=0, has_side_effects=True),
+        compiler_params=pltpu.CompilerParams(collective_id=0, has_side_effects=True, vmem_limit_bytes=62 * 2**20),
         name="gather",
     )(queries, out_grad, keys, values)
 
@@ -193,11 +177,28 @@
 
 
 def attend_kernel(
-    len_ref, owner_ref, q_ref, g_ref, k_ref, v_ref, o_ref, dq_ref, dk_ref, dv_ref, pair_ref,
+    second, len_ref, col_ref, *refs,
+):
+    if second:
+        old_dk_ref, old_dv_ref, *refs = refs
+    else:
+        owner_ref, *refs = refs
+    q0_ref, g0_ref, q1_ref, g1_ref, k_ref, v_ref, r0_ref, r1_ref, dk_ref, dv_ref, *refs = refs
+    if not second:
+        pair_ref, *refs = refs
+    attend_block(
+        second, len_ref, None if second else owner_ref, (q0_ref, q1_ref), (g0_ref, g1_ref), k_ref, v_ref,
+        (r0_ref, r1_ref), dk_ref, dv_ref, None if second else pair_ref,
+        (old_dk_ref, old_dv_ref) if second else None, *refs,
+    )
+
+
+def attend_block(
+    second, len_ref, owner_ref, q_refs, g_refs, k_ref, v_ref, r_refs, dk_ref, dv_ref, pair_ref, old,
     kt_ref, vt_ref, p_ref, qt_ref, gt_ref, qn_ref, gn_ref, dka_ref, dva_ref, ds_ref, acc_ref,
 ):
     blk = pl.program_id(0)
-    block, width = q_ref.shape
+    block, width = q_refs[0].shape
     heads = width // HD
     cols = block * heads
     tokens = k_ref.shape[0]
@@ -205,9 +206,18 @@
     f32, bf16 = jnp.float32, jnp.bfloat16
     scale = 1.0 / math.sqrt(HD)
     scale2 = scale * math.log2(math.e)
-    _, y, _ = place()
+    x, y, core = place()
+    if second:
+        x = 1 - x
     per_chip = tokens // (2 * YS)
-    per_range = pl.num_programs(0) // 2
+    per_core = pl.num_programs(0) // 2
+    chip_first = (x * YS + y) * per_chip
+    chip_start, end = jnp.int32(0), jnp.int32(0)
+    for d in range(docs):
+        end = end + len_ref[d]
+        chip_start = jnp.where(chip_first >= end, end, chip_start)
+    chunk_low = lax.div(chip_start, PASS)
+    chunk_high = lax.div(chip_first + per_chip, PASS)
 
     @pl.when(blk == 0)
     def _():
@@ -220,21 +230,24 @@
             dva_ref[rows, :] = jnp.zeros((PASS, HD), f32)
             return carry
 
-        lax.fori_loop(0, tokens // PASS, prepare, 0)
-        blocks = owner_ref.shape[1]
-        block_rows = tokens // blocks
-        shape = (block_rows, blocks)
-        pos = lax.broadcasted_iota(jnp.int32, shape, 1) * block_rows
-        pos = pos + lax.broadcasted_iota(jnp.int32, shape, 0)
-        begin, end = jnp.zeros(shape, jnp.int32), jnp.int32(0)
-        for d in range(docs):
-            end = end + len_ref[d]
-            begin = jnp.where(pos >= end, end, begin)
-        counts = (pos - begin + 1).astype(f32)
-        counts = jnp.where(owner_ref[...] == lax.axis_index("context"), counts, 0.0)
-        pair_ref[0] = jnp.sum(counts)
-
-    first = (blk // per_range) * (tokens // 2) + y * per_chip + lax.rem(blk, per_range) * block
+        lax.fori_loop(chunk_low, chunk_high, prepare, 0)
+        if not second:
+            blocks = owner_ref.shape[1]
+            block_rows = tokens // blocks
+            shape = (block_rows, blocks)
+            pos = lax.broadcasted_iota(jnp.int32, shape, 1) * block_rows
+            pos = pos + lax.broadcasted_iota(jnp.int32, shape, 0)
+            begin, end = jnp.zeros(shape, jnp.int32), jnp.int32(0)
+            for d in range(docs):
+                end = end + len_ref[d]
+                begin = jnp.where(pos >= end, end, begin)
+            counts = (pos - begin + 1).astype(f32)
+            counts = jnp.where(owner_ref[...] == lax.axis_index("context"), counts, 0.0)
+            pair_ref[0] = jnp.sum(counts)
+
+    half = lax.div(blk, per_core)
+    row_core = jnp.where(half == 0, core, 1 - core)
+    first = chip_first + row_core * (per_chip // 2) + lax.rem(blk, per_core) * block
     row_pos = first + lax.rem(lax.broadcasted_iota(jnp.int32, (1, cols), 1), block)
     row_start = jnp.zeros((1, cols), jnp.int32)
     first_start, last_start, end = jnp.int32(0), jnp.int32(0), jnp.int32(0)
@@ -249,11 +262,25 @@
     own_keys = kt_ref[:, rows_at(first, block)].astype(f32)
     shift = []
     for h in range(heads):
-        q_t = q_ref[:, h * HD : (h + 1) * HD].T
-        qt_ref[:, h * block : (h + 1) * block] = q_t
-        gt_ref[:, h * block : (h + 1) * block] = g_ref[:, h * HD : (h + 1) * HD].T
+        for n in range(2):
+
+            @pl.when(half == n)
+            def _(n=n, h=h):
+                qt_ref[:, h * block : (h + 1) * block] = q_refs[n][:, h * HD : (h + 1) * HD].T
+                gt_ref[:, h * block : (h + 1) * block] = g_refs[n][:, h * HD : (h + 1) * HD].T
+
+        q_t = qt_ref[:, h * block : (h + 1) * block]
         shift.append(jnp.sum(q_t.astype(f32) * own_keys, axis=0, keepdims=True) * scale2)
     shift = jnp.concatenate(shift, axis=1)
+
+    def keep(result, at):
+        for n in range(2):
+
+            @pl.when(half == n)
+            def _(n=n):
+                for h in range(heads):
+                    cut = result[h * block : (h + 1) * block, :]
+                    r_refs[n][:, (at + h) * HD : (at + h + 1) * HD] = cut
 
     def key_rows(t, count):
         return pl.ds(pl.multiple_of(t * TILE, TILE), count)
@@ -328,9 +355,7 @@
     grad_dot = jnp.sum(out.astype(f32) * grad_t, axis=0, keepdims=True)
     gn_ref[...] = (grad_t * inverse).astype(bf16).T
     qn_ref[...] = (qt_ref[...].astype(f32) * inverse).astype(bf16).T
-    out = out.T
-    for h in range(heads):
-        o_ref[:, h * HD : (h + 1) * HD] = out[h * block : (h + 1) * block, :]
+    keep(out.T, 0)
     acc_ref[0:HD, :] = jnp.zeros((HD, cols), f32)
 
     def backward(t, rows, last):
@@ -343,80 +368,113 @@
 
     sweep(backward)
     query_grad = (acc_ref[0:HD, :] * (inverse * scale)).astype(bf16).T
-    for h in range(heads):
-        dq_ref[:, h * HD : (h + 1) * HD] = query_grad[h * block : (h + 1) * block, :]
+    keep(query_grad, heads)
 
     @pl.when(blk == pl.num_programs(0) - 1)
     def _():
         def finish(i, carry):
             rows = rows_at(i * PASS, PASS)
-            dk_ref[rows, :] = (dka_ref[rows, :] * scale).astype(bf16)
-            dv_ref[rows, :] = dva_ref[rows, :].astype(bf16)
+            inside = (i >= chunk_low) & (i < chunk_high)
+            for n, (sums, out_ref, factor) in enumerate(((dka_ref, dk_ref, scale), (dva_ref, dv_ref, 1.0))):
+
+                @pl.when(inside)
+                def _(n=n, sums=sums, out_ref=out_ref, factor=factor):
+                    total = sums[rows, :] * factor
+                    if second:
+                        total = total + old[n][rows, :].astype(f32)
+                    out_ref[rows, :] = total.astype(bf16)
+
+                @pl.when(jnp.logical_not(inside))
+                def _(n=n, out_ref=out_ref):
+                    out_ref[rows, :] = old[n][rows, :] if second else jnp.zeros((PASS, HD), bf16)
+
             return carry
 
         lax.fori_loop(0, tokens // PASS, finish, 0)
 
 
-def attend(queries, out_grad, keys, values, lengths, block_owner):
-    rows, width = queries.shape
+def attend(rows, cols, keys, values, lengths, block_owner=None, old=None):
+    second = old is not None
     tokens = keys.shape[0]
-    cols = QBLOCK * (width // HD)
+    shard = rows[0].shape[0]
+    per_core = shard // QBLOCK
+    width = HEADS_HERE * HD
     span = ((DOC_MAX + QBLOCK + TILE - 2) // TILE + 1) * TILE
-    row_spec = pl.BlockSpec((QBLOCK, width), lambda i, *_: (i, 0))
+    qcols = QBLOCK * HEADS_HERE
+
+    def own(i):
+        return jnp.minimum(i, per_core - 1)
+
+    def other(i):
+        return jnp.maximum(i - per_core, 0)
+
+    def row_spec(n):
+        where = own if n < 2 else other
+        return pl.BlockSpec((QBLOCK, width), lambda i, _, col: (where(i), col[n]))
+
     full_spec = pl.BlockSpec((tokens, HD), lambda i, *_: (0, 0))
-    owner_spec = pl.BlockSpec((1, block_owner.shape[0]), lambda i, *_: (0, 0))
     bf16, f32 = jnp.bfloat16, jnp.float32
+    if second:
+        extra, extra_specs = list(old), [full_spec] * 2
+    else:
+        extra = [block_owner.reshape(1, -1)]
+        extra_specs = [pl.BlockSpec((1, block_owner.shape[0]), lambda i, *_: (0, 0))]
+    out_specs = [
+        pl.BlockSpec((QBLOCK, 2 * width), lambda i, *_: (own(i), 0)),
+        pl.BlockSpec((QBLOCK, 2 * width), lambda i, *_: (other(i), 0)),
+        full_spec, full_spec,
+    ]
+    out_shape = [
+        jax.ShapeDtypeStruct((shard, 2 * width), bf16),
+        jax.ShapeDtypeStruct((shard, 2 * width), bf16),
+        jax.ShapeDtypeStruct((tokens, HD), bf16),
+        jax.ShapeDtypeStruct((tokens, HD), bf16),
+    ]
+    if not second:
+        out_specs.append(pl.BlockSpec(memory_space=pltpu.SMEM))
+        out_shape.append(jax.ShapeDtypeStruct((1,), f32))
     return pl.pallas_call(
-        attend_kernel,
+        functools.partial(attend_kernel, second),
         grid_spec=pltpu.PrefetchScalarGridSpec(
-            num_scalar_prefetch=1,
-            grid=(rows // QBLOCK,),
-            in_specs=[owner_spec, row_spec, row_spec, full_spec, full_spec],
-            out_specs=[
-                row_spec, row_spec, full_spec, full_spec, pl.BlockSpec(memory_space=pltpu.SMEM),
-            ],
+            num_scalar_prefetch=2,
+            grid=(2 * per_core,),
+            in_specs=extra_specs + [row_spec(n) for n in range(4)] + [full_spec, full_spec],
+            out_specs=out_specs,
             scratch_shapes=[
                 pltpu.VMEM((HD, tokens), bf16),
                 pltpu.VMEM((HD + ONES, tokens), bf16),
-                pltpu.VMEM((span, cols), bf16),
-                pltpu.VMEM((HD, cols), bf16),
-                pltpu.VMEM((HD, cols), bf16),
-                pltpu.VMEM((cols, HD), bf16),
-                pltpu.VMEM((cols, HD), bf16),
+                pltpu.VMEM((span, qcols), bf16),
+                pltpu.VMEM((HD, qcols), bf16),
+                pltpu.VMEM((HD, qcols), bf16),
+                pltpu.VMEM((qcols, HD), bf16),
+                pltpu.VMEM((qcols, HD), bf16),
                 pltpu.VMEM((tokens, HD), f32),
                 pltpu.VMEM((tokens, HD), f32),
-                pltpu.VMEM((SPAN * TILE, cols), bf16),
-                pltpu.VMEM((HD + ONES, cols), f32),
+                pltpu.VMEM((SPAN * TILE, qcols), bf16),
+                pltpu.VMEM((HD + ONES, qcols), f32),
             ],
         ),
-        out_shape=[
-            jax.ShapeDtypeStruct((rows, width), bf16),
-            jax.ShapeDtypeStruct((rows, width), bf16),
-            jax.ShapeDtypeStruct((tokens, HD), bf16),
-            jax.ShapeDtypeStruct((tokens, HD), bf16),
-            jax.ShapeDtypeStruct((1,), f32),
-        ],
+        out_shape=out_shape,
+        cost_estimate=pl.CostEstimate(flops=2 * 10**10, bytes_accessed=2 * 10**7, transcendentals=5 * 10**6),
         compiler_params=pltpu.CompilerParams(vmem_limit_bytes=62 * 2**20),
-        name="attend",
-    )(lengths, block_owner.reshape(1, -1), queries, out_grad, keys, values)
+        name="attend_far" if second else "attend_near",
+    )(lengths, cols, *extra, *rows, keys, values)
 
 
 def scatter_kernel(
-    oa_ref, qa_ref, dk_ref, dv_ref, o_ref, q_ref, key_ref, value_ref,
+    dk_ref, dv_ref, rows_ref, back_ref, key_ref, value_ref,
     part, from_core, from_far, from_near, from_x,
-    own_sem, part_sem, core_send, core_recv, far_send, far_recv, near_send, near_recv,
+    part_sem, core_send, core_recv, far_send, far_recv, near_send, near_recv,
     x_send, x_recv, row_send, row_recv,
 ):
     x, y, core = place()
     shard = key_ref.shape[0]
     half = shard // 2
-    width = oa_ref.shape[1]
     up, down, far = (y + 1) % YS, (y + YS - 1) % YS, (y + 2) % YS
-    slot = x * 2 + core
     x_rank = rank_of(1 - x, y, core)
     core_rank = rank_of(x, y, 1 - core)
     up_rank, down_rank = rank_of(x, up, core), rank_of(x, down, core)
-    started, own = [], []
+    started = []
 
     def send(src, dst, send_sem, recv_sem, rank):
         copy = remote(src, dst, send_sem, recv_sem, rank)
@@ -441,24 +499,7 @@
             rows = rows_at(rank_of(sx, sy, 1 - core) * shard, shard)
             send(src.at[rows], from_core.at[a, n], core_send.at[a, n], core_recv.at[a, n], core_rank)
 
-    def head_cols(owner):
-        return pl.ds(pl.multiple_of(owner * width, width), width)
-
-    for a, (src, dst) in enumerate(((oa_ref, o_ref), (qa_ref, q_ref))):
-        copy = pltpu.make_async_copy(
-            src.at[rows_at(slot * shard, shard)], dst.at[:, head_cols(slot)], own_sem.at[a]
-        )
-        copy.start()
-        own.append(copy)
-        for d, (dx, dc) in enumerate(((0, 1), (1, 0), (1, 1))):
-            tx, tc = (x + dx) % 2, (core + dc) % 2
-            send(
-                src.at[rows_at((tx * 2 + tc) * shard, shard)],
-                dst.at[:, head_cols(slot)],
-                row_send.at[a, d],
-                row_recv.at[a, d],
-                rank_of(tx, y, tc),
-            )
+    send(rows_ref, back_ref, row_send, row_recv, core_rank)
 
     def add(ref, other):
         ref[...] = (ref[...].astype(jnp.float32) + other[...].astype(jnp.float32)).astype(jnp.bfloat16)
@@ -511,19 +552,14 @@
     for a, dst in enumerate((key_ref, value_ref)):
         landed(from_x.at[a], x_recv.at[a])
         dst[...] = (part[a, 7].astype(jnp.float32) + from_x[a].astype(jnp.float32)).astype(jnp.bfloat16)
-    for a, dst in enumerate((o_ref, q_ref)):
-        for d, (dx, dc) in enumerate(((0, 1), (1, 0), (1, 1))):
-            tx, tc = (x + dx) % 2, (core + dc) % 2
-            landed(dst.at[:, head_cols(tx * 2 + tc)], row_recv.at[a, d])
-    for copy in own:
-        copy.wait()
+    landed(back_ref, row_recv)
     for copy in started:
         copy.wait_send()
 
 
-def scatter(out_rows, query_rows, key_terms, value_terms, ranks):
-    rows, width = out_rows.shape
-    shard = rows // GROUP
+def scatter(key_terms, value_terms, rows, ranks):
+    tokens = key_terms.shape[0]
+    shard = tokens // ranks
     half = shard // 2
     bf16 = jnp.bfloat16
     any_spec = pl.BlockSpec(memory_space=pl.ANY)
@@ -531,11 +567,10 @@
     dma = pltpu.SemaphoreType.DMA
     return pl.pallas_call(
         scatter_kernel,
-        in_specs=[any_spec] * 4,
-        out_specs=[any_spec, any_spec, vmem_spec, vmem_spec],
+        in_specs=[any_spec] * 3,
+        out_specs=[any_spec, vmem_spec, vmem_spec],
         out_shape=[
-            jax.ShapeDtypeStruct((shard, width * GROUP), bf16),
-            jax.ShapeDtypeStruct((shard, width * GROUP), bf16),
+            jax.ShapeDtypeStruct(rows.shape, bf16),
             jax.ShapeDtypeStruct((shard, HD), bf16),
             jax.ShapeDtypeStruct((shard, HD), bf16),
         ],
@@ -545,23 +580,77 @@
             pltpu.VMEM((2, 2, 2, half, HD), bf16),
             pltpu.VMEM((2, 2, 2, shard, HD), bf16),
             pltpu.VMEM((2, shard, HD), bf16),
-            dma((2,)), dma((2, 8)), dma((2, 8)), dma((2, 8)), dma((2, 2, 2)), dma((2, 2, 2)),
-            dma((2, 2, 2, 2)), dma((2, 2, 2, 2)), dma((2,)), dma((2,)), dma((2, 3)), dma((2, 3)),
+            dma((2, 8)), dma((2, 8)), dma((2, 8)), dma((2, 2, 2)), dma((2, 2, 2)),
+            dma((2, 2, 2, 2)), dma((2, 2, 2, 2)), dma((2,)), dma((2,)), dma, dma,
         ],
+        cost_estimate=pl.CostEstimate(flops=2 * 10**7, bytes_accessed=2 * 10**7, transcendentals=0),
         compiler_params=pltpu.CompilerParams(
-            collective_id=1, has_side_effects=True, vmem_limit_bytes=40 * 2**20
+            collective_id=1, has_side_effects=True, vmem_limit_bytes=62 * 2**20
         ),
         name="scatter",
-    )(out_rows, query_rows, key_terms, value_terms)
+    )(key_terms, value_terms, rows)
+
+
+def place_kernel(a_ref, b_ref, c_ref, d_ref, o_ref, q_ref, sem):
+    x, _, core = place()
+    width = a_ref.shape[1] // 2
+    copies = []
+    for n, (ref, slot) in enumerate((
+        (a_ref, x * 2 + core), (b_ref, x * 2 + 1 - core),
+        (c_ref, (1 - x) * 2 + core), (d_ref, (1 - x) * 2 + 1 - core),
+    )):
+        cols = pl.ds(pl.multiple_of(slot * width, width), width)
+        for a, dst in enumerate((o_ref, q_ref)):
+            copy = pltpu.make_async_copy(ref.at[:, pl.ds(a * width, width)], dst.at[:, cols], sem.at[n, a])
+            copy.start()
+            copies.append(copy)
+    for copy in copies:
+        copy.wait()
+
+
+def place_columns(pieces):
+    shard, width = pieces[0].shape
+    shape = jax.ShapeDtypeStruct((shard, width * 2), jnp.bfloat16)
+    any_spec = pl.BlockSpec(memory_space=pl.ANY)
+    return pl.pallas_call(
+        place_kernel,
+        in_specs=[any_spec] * 4,
+        out_specs=[any_spec] * 2,
+        out_shape=[shape, shape],
+        scratch_shapes=[pltpu.SemaphoreType.DMA((4, 2))],
+        compiler_params=pltpu.CompilerParams(vmem_limit_bytes=62 * 2**20),
+        name="place",
+    )(*pieces)
 
 
 def body(queries, key_rows, values, out_grad, lengths, block_owner):
     ranks = lax.axis_size("context")
-    queries, out_grad, keys, values = gather(queries, out_grad, key_rows, values, ranks)
-    out, query_grad, key_terms, value_terms, pair_count = attend(
-        queries, out_grad, keys, values, lengths, block_owner
+    x, _, core = place()
+    width = queries.shape[1] // GROUP
+    same = [(rank_of(a, b, c), rank_of(1 - a, b, c)) for a in range(2) for b in range(YS) for c in range(2)]
+    cross = [(rank_of(a, b, c), rank_of(1 - a, b, 1 - c)) for a in range(2) for b in range(YS) for c in range(2)]
+
+    def heads_of(slot):
+        cut = [lax.dynamic_slice_in_dim(t, slot * width, width, 1) for t in (queries, out_grad)]
+        return jnp.concatenate(cut, axis=1)
+
+    far_same = lax.ppermute(heads_of((1 - x) * 2 + core), "context", same)
+    far_cross = lax.ppermute(heads_of((1 - x) * 2 + 1 - core), "context", cross)
+    near, keys, all_values = gather(queries, out_grad, key_rows, values, ranks)
+    slot = (x * 2 + core).astype(jnp.int32)
+    zero, one = jnp.int32(0), jnp.int32(1)
+    own_rows, near_rows, dk, dv, pair_count = attend(
+        (queries, out_grad, near, near), jnp.stack([slot, slot, zero, one]), keys, all_values, lengths,
+        block_owner=block_owner,
     )
-    out, query_grad, key_grad, value_grad = scatter(out, query_grad, key_terms, value_terms, ranks)
+    same_rows, cross_rows, dk, dv = attend(
+        (far_same, far_same, far_cross, far_cross), jnp.stack([zero, one, zero, one]), keys, all_values, lengths,
+        old=(dk, dv),
+    )
+    same_rows = lax.ppermute(same_rows, "context", same)
+    cross_rows = lax.ppermute(cross_rows, "context", cross)
+    near_rows, key_grad, value_grad = scatter(dk, dv, near_rows, ranks)
+    out, query_grad = place_columns((own_rows, near_rows, same_rows, cross_rows))
     return out, query_grad, key_grad, value_grad, pair_count
 
 

time: 137 us -> 210 us (1.53)
  the two profiles are of different devices: /device:TPU:64 before, /device:TPU:32 now
where the time goes in v2:
time: 210 us
  Pallas kernels  201 us (96%)
  local copies, waits for them, and re-layouts  4.34 us (2%)
  starting transfers between devices  3.54 us (2%)
    pallas_call x1, Pallas kernels, place_columns(): pl.pallas_call(place_kernel, in_specs=[any_spec] * 4, out_specs=[any_spec...  64.7 us
    pallas_call x2, Pallas kernels, attend(): pl.pallas_call(functools.partial(attend_kernel, second), grid_spec=pltpu....  60.8 us
    pallas_call x1, Pallas kernels, gather(): pl.pallas_call(gather_kernel, in_specs=[any_spec] * 4, out_specs=[any_spe...  44 us
    pallas_call x1, Pallas kernels, scatter(): pl.pallas_call(scatter_kernel, in_specs=[any_spec] * 3, out_specs=[any_sp...  31.3 us
  transfers between devices with their start and end apart: 4, of which 0 were waited for; matrix products, arithmetic and copies ran while one was open for 0% of the time, Pallas kernels for 43%

profile of v2, /device:TPU:32, one launch (start us, length us, event | category | flops | bytes accessed | tf_op | source)
XLA Modules:
  0.0 210.2 jit_solution(12774831134892200716)
XLA Ops:
  0.7 1.3 constant_dynamic-slice_fusion
  2.0 1.6 collective-permute-start
  3.6 0.1 collective-permute-start.1
  3.7 44.0 %gather.1 = (bf16[512,512]{1,0:T(8,128)(2,1)}, bf16[8192,128]{1,0:T(8,128)(2,1)}, bf16[8192,128]{1,0:T(8,128)(2,1)}) custom-call(bf16[512,1024]{1,0:T(8,128)(2,1)} %refs_1_.1, bf16[512,1024]{1,0:T(8,128)(2,1)} %refs_2_.1, bf16[512,128]{1,0:T(8,128)(2,1)} %k_ref.1, bf16[512,128]{1,0:T(8,128)(2,1)} %v_ref.1), custom_call_target="tpu_custom_call" | custom-call | tf_op jit(solution)/shard_map/gather/pallas_call | solution.py:158
  47.7 0.6 pad_add_fusion.col_ref
  48.3 14.5 %attend_near.1 = (bf16[512,512]{1,0:T(8,128)(2,1)}, bf16[512,512]{1,0:T(8,128)(2,1)}, bf16[8192,128]{1,0:T(8,128)(2,1)}, bf16[8192,128]{1,0:T(8,128)(2,1)}, f32[1]{0:T(128)}) custom-call(s32[16]{0:T(128)} %len_ref.3, s32[4]{0:T(128)} %pad_add_fusion.col_ref, s32[1,128]{1,0:T(1,128)} %bitcast.2, bf16[512,1024]{1,0:T(8,128)(2,1)} %refs_1_.1, ...), custom_call_target="tpu_custom_call" | custom-call | flops 20000000000 | bytes 20000000 | tf_op jit(solution)/shard_map/attend_near/pallas_call | solution.py:436
  62.8 0.0 collective-permute-done.refs_2_.refs_3_
  62.9 0.0 copy-start.4
  62.9 0.0 collective-permute-done.1.refs_4_.refs_5_
  62.9 0.8 copy-done.4
  63.7 46.3 %attend_far.1 = (bf16[512,512]{1,0:T(8,128)(2,1)}, bf16[512,512]{1,0:T(8,128)(2,1)}, bf16[8192,128]{1,0:T(8,128)(2,1)}, bf16[8192,128]{1,0:T(8,128)(2,1)}) custom-call(s32[16]{0:T(128)} %len_ref.3, s32[4]{0:T(128)} %constant.40.clone.1.col_ref, bf16[8192,128]{1,0:T(8,128)(2,1)} %get-tuple-element.26.refs_0_, bf16[8192,128]{1,0:T(8,128)(2,1)} %get-tuple-element.27.refs_1_, ...), custom_call_target="tpu_custom_call" | custom-call | flops 20000000000 | bytes 20000000 | tf_op jit(solution)/shard_map/attend_far/pallas_call | solution.py:436
  110.0 1.4 collective-permute-start.2
  111.4 0.5 collective-permute-start.3
  111.8 31.3 %scatter.1 = (bf16[512,512]{1,0:T(8,128)(2,1)}, bf16[512,128]{1,0:T(8,128)(2,1)}, bf16[512,128]{1,0:T(8,128)(2,1)}) custom-call(bf16[8192,128]{1,0:T(8,128)(2,1)} %get-tuple-element.28.dk_ref, bf16[8192,128]{1,0:T(8,128)(2,1)} %get-tuple-element.29.dv_ref, bf16[512,512]{1,0:T(8,128)(2,1)} %get-tuple-element.30.rows_ref), custom_call_target="tpu_custom_call" | custom-call | flops 20000000 | bytes 20000000 | tf_op jit(solution)/shard_map/scatter/pallas_call | solution.py:568
  143.1 0.0 copy-start.3
  143.1 0.0 copy-start.2
  143.1 0.0 collective-permute-done.2.c_ref
  143.1 0.0 copy-start
  143.1 0.0 collective-permute-done.3.d_ref
  143.2 0.0 copy-start.1
  143.2 0.8 copy-done
  143.9 0.2 copy-done.1
  144.1 64.7 %place.1 = (bf16[512,1024]{1,0:T(8,128)(2,1)}, bf16[512,1024]{1,0:T(8,128)(2,1)}) custom-call(bf16[512,512]{1,0:T(8,128)(2,1)} %get-tuple-element.25.a_ref, bf16[512,512]{1,0:T(8,128)(2,1)} %get-tuple-element.31.b_ref, bf16[512,512]{1,0:T(8,128)(2,1)} %copy-done, bf16[512,512]{1,0:T(8,128)(2,1)} %copy-done.1), custom_call_target="tpu_custom_call" | custom-call | tf_op jit(solution)/shard_map/place/pallas_call | solution.py:615
  208.8 0.0 copy-done.3
  208.8 0.7 copy.13
  209.5 0.0 copy-done.2
  209.5 0.7 copy.14
  (2 shorter events, 0.1 us)
Async XLA Ops:
  2.0 60.9 %collective-permute-start = (bf16[512,512]{1,0:T(8,128)(2,1)S(1)}, bf16[512,512]{1,0:T(8,128)(2,1)S(1)}, u32[]{:S(2)}, u32[]{:S(2)}) collective-permute-start(bf16[512,512]{1,0:T(8,128)(2,1)S(1)} %pad_maximum_fusion), channel_id=1, source_target_pairs={{0,8},{1,9},{2,10},{3,11},{4,12},{5,13},{6,14},{7,15},{8,0},{9,1},... | collective-permute-start | bytes 1572872 | tf_op jit(solution)/shard_map/ppermute | solution.py:637
  3.6 59.3 %collective-permute-start.1 = (bf16[512,512]{1,0:T(8,128)(2,1)S(1)}, bf16[512,512]{1,0:T(8,128)(2,1)}, u32[]{:S(2)}, u32[]{:S(2)}) collective-permute-start(bf16[512,512]{1,0:T(8,128)(2,1)S(1)} %pad_maximum_fusion.1), channel_id=1, source_target_pairs={{0,9},{1,8},{2,11},{3,10},{4,13},{5,12},{6,15},{7,14},{8,1},{9,0},... | collective-permute-start | bytes 1572872 | tf_op jit(solution)/shard_map/ppermute | solution.py:638
  62.9 0.8 copy-start.4
  110.0 33.2 %collective-permute-start.2 = (bf16[512,512]{1,0:T(8,128)(2,1)}, bf16[512,512]{1,0:T(8,128)(2,1)S(1)}, u32[]{:S(2)}, u32[]{:S(2)}) collective-permute-start(bf16[512,512]{1,0:T(8,128)(2,1)} %get-tuple-element.32), channel_id=1, source_target_pairs={{0,8},{1,9},{2,10},{3,11},{4,12},{5,13},{6,14},{7,15},{8,0},{9,1},... | collective-permute-start | bytes 1572872 | tf_op jit(solution)/shard_map/ppermute | solution.py:650
  111.4 31.8 %collective-permute-start.3 = (bf16[512,512]{1,0:T(8,128)(2,1)}, bf16[512,512]{1,0:T(8,128)(2,1)S(1)}, u32[]{:S(2)}, u32[]{:S(2)}) collective-permute-start(bf16[512,512]{1,0:T(8,128)(2,1)} %get-tuple-element.33), channel_id=1, source_target_pairs={{0,9},{1,8},{2,11},{3,10},{4,13},{5,12},{6,15},{7,14},{8,1},{9,0},... | collective-permute-start | bytes 1572872 | tf_op jit(solution)/shard_map/ppermute | solution.py:651
  143.1 65.7 %copy-start.3 = (bf16[512,128]{1,0:T(8,128)(2,1)S(1)}, bf16[512,128]{1,0:T(8,128)(2,1)}, u32[]{:S(2)}) copy-start(bf16[512,128]{1,0:T(8,128)(2,1)} %get-tuple-element.52) | copy-start | bytes 393220
  143.1 66.4 %copy-start.2 = (bf16[512,128]{1,0:T(8,128)(2,1)S(1)}, bf16[512,128]{1,0:T(8,128)(2,1)}, u32[]{:S(2)}) copy-start(bf16[512,128]{1,0:T(8,128)(2,1)} %get-tuple-element.53) | copy-start | bytes 393220
  143.1 0.8 copy-start
  143.2 1.0 copy-start.1

commit v3 on v2

--- a/solution.py
+++ b/solution.py
@@ -43,7 +43,7 @@
     )
 
 
-def enter(x, y, core):
+def enter(x, y, core, rows=False):
     barrier = pltpu.get_barrier_semaphore()
     others = [
         rank_of(x, y, 1 - core),
@@ -51,6 +51,8 @@
         rank_of(x, (y + 1) % YS, core),
         rank_of(x, (y + YS - 1) % YS, core),
     ]
+    if rows:
+        others.append(rank_of(1 - x, y, 1 - core))
     for other in others:
         pl.semaphore_signal(barrier, inc=1, device_id={"context": other}, device_id_type=MESH)
     pl.semaphore_wait(barrier, len(others))
@@ -72,7 +74,7 @@
     x_rank = rank_of(1 - x, y, core)
     core_rank = rank_of(x, y, 1 - core)
     up_rank, down_rank = rank_of(x, up, core), rank_of(x, down, core)
-    enter(x, y, core)
+    enter(x, y, core, rows=True)
     started = []
 
     def send(src, dst, send_sem, recv_sem, rank):
@@ -96,11 +98,13 @@
         own.append(copy)
 
     for a, src in enumerate((q_ref, g_ref)):
-        cols = pl.ds(pl.multiple_of((x * 2 + 1 - core) * width, width), width)
-        send(
-            src.at[:, cols], rows_ref.at[:, pl.ds(a * width, width)],
-            row_send.at[a], row_recv.at[a], core_rank,
-        )
+        for d in range(1, GROUP):
+            tx, tc = (x + d // 2) % 2, (core + d % 2) % 2
+            cols = pl.ds(pl.multiple_of((tx * 2 + tc) * width, width), width)
+            send(
+                src.at[:, cols], rows_ref.at[pl.ds((d - 1) * shard, shard), pl.ds(a * width, width)],
+                row_send.at[a, d - 1], row_recv.at[a, d - 1], rank_of(tx, y, tc),
+            )
 
     def forward(a, n, ref, rows, rank, relay):
         send(ref.at[rows], ref.at[rows], relay[0].at[a, n], relay[1].at[a, n], rank)
@@ -142,7 +146,8 @@
             for h in range(2):
                 landed(dst.at[half_rows(sx, far, oc, h)], core_recv.at[a, 5 + n + h])
     for a in range(2):
-        landed(rows_ref.at[:, pl.ds(a * width, width)], row_recv.at[a])
+        for d in range(1, GROUP):
+            landed(rows_ref.at[pl.ds((d - 1) * shard, shard), pl.ds(a * width, width)], row_recv.at[a, d - 1])
     for copy in own:
         copy.wait()
     for copy in started:
@@ -160,12 +165,12 @@
         in_specs=[any_spec] * 4,
         out_specs=[any_spec] * 3,
         out_shape=[
-            jax.ShapeDtypeStruct((shard, 2 * width), bf16),
+            jax.ShapeDtypeStruct(((GROUP - 1) * shard, 2 * width), bf16),
             jax.ShapeDtypeStruct((ranks * shard, HD), bf16),
             jax.ShapeDtypeStruct((ranks * shard, HD), bf16),
         ],
         scratch_shapes=[
-            dma((2,)), dma((2, 9)), dma((2, 9)), dma((2, 10)), dma((2, 10)), dma((2,)), dma((2,)),
+            dma((2,)), dma((2, 9)), dma((2, 9)), dma((2, 10)), dma((2, 10)), dma((2, 3)), dma((2, 3)),
         ],
         compiler_params=pltpu.CompilerParams(collective_id=0, has_side_effects=True, vmem_limit_bytes=62 * 2**20),
         name="gather",
@@ -177,28 +182,13 @@
 
 
 def attend_kernel(
-    second, len_ref, col_ref, *refs,
-):
-    if second:
-        old_dk_ref, old_dv_ref, *refs = refs
-    else:
-        owner_ref, *refs = refs
-    q0_ref, g0_ref, q1_ref, g1_ref, k_ref, v_ref, r0_ref, r1_ref, dk_ref, dv_ref, *refs = refs
-    if not second:
-        pair_ref, *refs = refs
-    attend_block(
-        second, len_ref, None if second else owner_ref, (q0_ref, q1_ref), (g0_ref, g1_ref), k_ref, v_ref,
-        (r0_ref, r1_ref), dk_ref, dv_ref, None if second else pair_ref,
-        (old_dk_ref, old_dv_ref) if second else None, *refs,
-    )
-
-
-def attend_block(
-    second, len_ref, owner_ref, q_refs, g_refs, k_ref, v_ref, r_refs, dk_ref, dv_ref, pair_ref, old,
+    len_ref, slot_ref, owner_ref, q0_ref, g0_ref, q1_ref, g1_ref, k_ref, v_ref,
+    r0_ref, r1_ref, r2_ref, r3_ref, dk_ref, dv_ref, pair_ref,
     kt_ref, vt_ref, p_ref, qt_ref, gt_ref, qn_ref, gn_ref, dka_ref, dva_ref, ds_ref, acc_ref,
 ):
     blk = pl.program_id(0)
-    block, width = q_refs[0].shape
+    q_refs, g_refs, r_refs = (q0_ref, q1_ref), (g0_ref, g1_ref), (r0_ref, r1_ref, r2_ref, r3_ref)
+    block, width = q0_ref.shape
     heads = width // HD
     cols = block * heads
     tokens = k_ref.shape[0]
@@ -207,17 +197,17 @@
     scale = 1.0 / math.sqrt(HD)
     scale2 = scale * math.log2(math.e)
     x, y, core = place()
-    if second:
-        x = 1 - x
     per_chip = tokens // (2 * YS)
-    per_core = pl.num_programs(0) // 2
-    chip_first = (x * YS + y) * per_chip
-    chip_start, end = jnp.int32(0), jnp.int32(0)
-    for d in range(docs):
-        end = end + len_ref[d]
-        chip_start = jnp.where(chip_first >= end, end, chip_start)
-    chunk_low = lax.div(chip_start, PASS)
-    chunk_high = lax.div(chip_first + per_chip, PASS)
+    per_core = pl.num_programs(0) // GROUP
+
+    reach = []
+    for chip in (y, YS + y):
+        begin, end = jnp.int32(0), jnp.int32(0)
+        for d in range(docs):
+            end = end + len_ref[d]
+            begin = jnp.where(chip * per_chip >= end, end, begin)
+        reach.append((lax.div(begin, PASS), lax.div((chip + 1) * per_chip, PASS)))
+    reach[1] = (jnp.maximum(reach[1][0], reach[0][1]), reach[1][1])
 
     @pl.when(blk == 0)
     def _():
@@ -230,24 +220,25 @@
             dva_ref[rows, :] = jnp.zeros((PASS, HD), f32)
             return carry
 
-        lax.fori_loop(chunk_low, chunk_high, prepare, 0)
-        if not second:
-            blocks = owner_ref.shape[1]
-            block_rows = tokens // blocks
-            shape = (block_rows, blocks)
-            pos = lax.broadcasted_iota(jnp.int32, shape, 1) * block_rows
-            pos = pos + lax.broadcasted_iota(jnp.int32, shape, 0)
-            begin, end = jnp.zeros(shape, jnp.int32), jnp.int32(0)
-            for d in range(docs):
-                end = end + len_ref[d]
-                begin = jnp.where(pos >= end, end, begin)
-            counts = (pos - begin + 1).astype(f32)
-            counts = jnp.where(owner_ref[...] == lax.axis_index("context"), counts, 0.0)
-            pair_ref[0] = jnp.sum(counts)
-
-    half = lax.div(blk, per_core)
-    row_core = jnp.where(half == 0, core, 1 - core)
-    first = chip_first + row_core * (per_chip // 2) + lax.rem(blk, per_core) * block
+        for low_chunk, high_chunk in reach:
+            lax.fori_loop(low_chunk, high_chunk, prepare, 0)
+        blocks = owner_ref.shape[1]
+        block_rows = tokens // blocks
+        shape = (block_rows, blocks)
+        pos = lax.broadcasted_iota(jnp.int32, shape, 1) * block_rows
+        pos = pos + lax.broadcasted_iota(jnp.int32, shape, 0)
+        begin, end = jnp.zeros(shape, jnp.int32), jnp.int32(0)
+        for d in range(docs):
+            end = end + len_ref[d]
+            begin = jnp.where(pos >= end, end, begin)
+        counts = (pos - begin + 1).astype(f32)
+        counts = jnp.where(owner_ref[...] == lax.axis_index("context"), counts, 0.0)
+        pair_ref[0] = jnp.sum(counts)
+
+    part = lax.div(blk, per_core)
+    chip = lax.rem(x + lax.div(part, 2), 2) * YS + y
+    row_core = lax.rem(core + part, 2)
+    first = chip * per_chip + row_core * (per_chip // 2) + lax.rem(blk, per_core) * block
     row_pos = first + lax.rem(lax.broadcasted_iota(jnp.int32, (1, cols), 1), block)
     row_start = jnp.zeros((1, cols), jnp.int32)
     first_start, last_start, end = jnp.int32(0), jnp.int32(0), jnp.int32(0)
@@ -264,7 +255,7 @@
     for h in range(heads):
         for n in range(2):
 
-            @pl.when(half == n)
+            @pl.when((part > 0) == bool(n))
             def _(n=n, h=h):
                 qt_ref[:, h * block : (h + 1) * block] = q_refs[n][:, h * HD : (h + 1) * HD].T
                 gt_ref[:, h * block : (h + 1) * block] = g_refs[n][:, h * HD : (h + 1) * HD].T
@@ -274,9 +265,9 @@
     shift = jnp.concatenate(shift, axis=1)
 
     def keep(result, at):
-        for n in range(2):
-
-            @pl.when(half == n)
+        for n in range(GROUP):
+
+            @pl.when(part == n)
             def _(n=n):
                 for h in range(heads):
                     cut = result[h * block : (h + 1) * block, :]
@@ -374,72 +365,54 @@
     def _():
         def finish(i, carry):
             rows = rows_at(i * PASS, PASS)
-            inside = (i >= chunk_low) & (i < chunk_high)
-            for n, (sums, out_ref, factor) in enumerate(((dka_ref, dk_ref, scale), (dva_ref, dv_ref, 1.0))):
+            inside = jnp.bool_(False)
+            for low_chunk, high_chunk in reach:
+                inside = inside | ((i >= low_chunk) & (i < high_chunk))
+            for sums, out_ref, factor in ((dka_ref, dk_ref, scale), (dva_ref, dv_ref, 1.0)):
 
                 @pl.when(inside)
-                def _(n=n, sums=sums, out_ref=out_ref, factor=factor):
-                    total = sums[rows, :] * factor
-                    if second:
-                        total = total + old[n][rows, :].astype(f32)
-                    out_ref[rows, :] = total.astype(bf16)
+                def _(sums=sums, out_ref=out_ref, factor=factor):
+                    out_ref[rows, :] = (sums[rows, :] * factor).astype(bf16)
 
                 @pl.when(jnp.logical_not(inside))
-                def _(n=n, out_ref=out_ref):
-                    out_ref[rows, :] = old[n][rows, :] if second else jnp.zeros((PASS, HD), bf16)
+                def _(out_ref=out_ref):
+                    out_ref[rows, :] = jnp.zeros((PASS, HD), bf16)
 
             return carry
 
         lax.fori_loop(0, tokens // PASS, finish, 0)
 
 
-def attend(rows, cols, keys, values, lengths, block_owner=None, old=None):
-    second = old is not None
+def attend(queries, out_grad, rows, slot, keys, values, lengths, block_owner):
     tokens = keys.shape[0]
-    shard = rows[0].shape[0]
+    shard = queries.shape[0]
     per_core = shard // QBLOCK
     width = HEADS_HERE * HD
     span = ((DOC_MAX + QBLOCK + TILE - 2) // TILE + 1) * TILE
     qcols = QBLOCK * HEADS_HERE
 
-    def own(i):
-        return jnp.minimum(i, per_core - 1)
-
-    def other(i):
-        return jnp.maximum(i - per_core, 0)
-
-    def row_spec(n):
-        where = own if n < 2 else other
-        return pl.BlockSpec((QBLOCK, width), lambda i, _, col: (where(i), col[n]))
+    def own_spec():
+        return pl.BlockSpec((QBLOCK, width), lambda i, _, slot: (jnp.minimum(i, per_core - 1), slot[0]))
+
+    def other_spec(col):
+        return pl.BlockSpec((QBLOCK, width), lambda i, *_: (jnp.maximum(i - per_core, 0), col))
+
+    def result_spec(n):
+        return pl.BlockSpec((QBLOCK, 2 * width), lambda i, *_: (jnp.clip(i - n * per_core, 0, per_core - 1), 0))
 
     full_spec = pl.BlockSpec((tokens, HD), lambda i, *_: (0, 0))
     bf16, f32 = jnp.bfloat16, jnp.float32
-    if second:
-        extra, extra_specs = list(old), [full_spec] * 2
-    else:
-        extra = [block_owner.reshape(1, -1)]
-        extra_specs = [pl.BlockSpec((1, block_owner.shape[0]), lambda i, *_: (0, 0))]
-    out_specs = [
-        pl.BlockSpec((QBLOCK, 2 * width), lambda i, *_: (own(i), 0)),
-        pl.BlockSpec((QBLOCK, 2 * width), lambda i, *_: (other(i), 0)),
-        full_spec, full_spec,
-    ]
-    out_shape = [
-        jax.ShapeDtypeStruct((shard, 2 * width), bf16),
-        jax.ShapeDtypeStruct((shard, 2 * width), bf16),
-        jax.ShapeDtypeStruct((tokens, HD), bf16),
-        jax.ShapeDtypeStruct((tokens, HD), bf16),
-    ]
-    if not second:
-        out_specs.append(pl.BlockSpec(memory_space=pltpu.SMEM))
-        out_shape.append(jax.ShapeDtypeStruct((1,), f32))
+    owner_spec = pl.BlockSpec((1, block_owner.shape[0]), lambda i, *_: (0, 0))
     return pl.pallas_call(
-        functools.partial(attend_kernel, second),
+        attend_kernel,
         grid_spec=pltpu.PrefetchScalarGridSpec(
             num_scalar_prefetch=2,
-            grid=(2 * per_core,),
-            in_specs=extra_specs + [row_spec(n) for n in range(4)] + [full_spec, full_spec],
-            out_specs=out_specs,
+            grid=(GROUP * per_core,),
+            in_specs=[
+                owner_spec, own_spec(), own_spec(), other_spec(0), other_spec(1), full_spec, full_spec,
+            ],
+            out_specs=[result_spec(n) for n in range(GROUP)]
+            + [full_spec, full_spec, pl.BlockSpec(memory_space=pltpu.SMEM)],
             scratch_shapes=[
                 pltpu.VMEM((HD, tokens), bf16),
                 pltpu.VMEM((HD + ONES, tokens), bf16),
@@ -454,11 +427,13 @@
                 pltpu.VMEM((HD + ONES, qcols), f32),
             ],
         ),
-        out_shape=out_shape,
+        out_shape=[jax.ShapeDtypeStruct((shard, 2 * width), bf16)] * GROUP
+        + [jax.ShapeDtypeStruct((tokens, HD), bf16)] * 2
+        + [jax.ShapeDtypeStruct((1,), f32)],
         cost_estimate=pl.CostEstimate(flops=2 * 10**10, bytes_accessed=2 * 10**7, transcendentals=5 * 10**6),
         compiler_params=pltpu.CompilerParams(vmem_limit_bytes=62 * 2**20),
-        name="attend_far" if second else "attend_near",
-    )(lengths, cols, *extra, *rows, keys, values)
+        name="attend",
+    )(lengths, slot, block_owner.reshape(1, -1), queries, out_grad, rows, rows, keys, values)
 
 
 def scatter_kernel(
@@ -591,33 +566,26 @@
     )(key_terms, value_terms, rows)
 
 
-def place_kernel(a_ref, b_ref, c_ref, d_ref, o_ref, q_ref, sem):
+def place_kernel(a_ref, b_ref, c_ref, d_ref, o_ref, q_ref):
     x, _, core = place()
     width = a_ref.shape[1] // 2
-    copies = []
-    for n, (ref, slot) in enumerate((
-        (a_ref, x * 2 + core), (b_ref, x * 2 + 1 - core),
-        (c_ref, (1 - x) * 2 + core), (d_ref, (1 - x) * 2 + 1 - core),
-    )):
+    for d, ref in enumerate((a_ref, b_ref, c_ref, d_ref)):
+        slot = ((x + d // 2) % 2) * 2 + (core + d % 2) % 2
         cols = pl.ds(pl.multiple_of(slot * width, width), width)
-        for a, dst in enumerate((o_ref, q_ref)):
-            copy = pltpu.make_async_copy(ref.at[:, pl.ds(a * width, width)], dst.at[:, cols], sem.at[n, a])
-            copy.start()
-            copies.append(copy)
-    for copy in copies:
-        copy.wait()
+        o_ref[:, cols] = ref[:, :width]
+        q_ref[:, cols] = ref[:, width:]
 
 
 def place_columns(pieces):
     shard, width = pieces[0].shape
+    block = shard // 4
     shape = jax.ShapeDtypeStruct((shard, width * 2), jnp.bfloat16)
-    any_spec = pl.BlockSpec(memory_space=pl.ANY)
     return pl.pallas_call(
         place_kernel,
-        in_specs=[any_spec] * 4,
-        out_specs=[any_spec] * 2,
+        grid=(shard // block,),
+        in_specs=[pl.BlockSpec((block, width), lambda i: (i, 0))] * GROUP,
+        out_specs=[pl.BlockSpec((block, width * 2), lambda i: (i, 0))] * 2,
         out_shape=[shape, shape],
-        scratch_shapes=[pltpu.SemaphoreType.DMA((4, 2))],
         compiler_params=pltpu.CompilerParams(vmem_limit_bytes=62 * 2**20),
         name="place",
     )(*pieces)
@@ -626,31 +594,18 @@
 def body(queries, key_rows, values, out_grad, lengths, block_owner):
     ranks = lax.axis_size("context")
     x, _, core = place()
-    width = queries.shape[1] // GROUP
-    same = [(rank_of(a, b, c), rank_of(1 - a, b, c)) for a in range(2) for b in range(YS) for c in range(2)]
-    cross = [(rank_of(a, b, c), rank_of(1 - a, b, 1 - c)) for a in range(2) for b in range(YS) for c in range(2)]
-
-    def heads_of(slot):
-        cut = [lax.dynamic_slice_in_dim(t, slot * width, width, 1) for t in (queries, out_grad)]
-        return jnp.concatenate(cut, axis=1)
-
-    far_same = lax.ppermute(heads_of((1 - x) * 2 + core), "context", same)
-    far_cross = lax.ppermute(heads_of((1 - x) * 2 + 1 - core), "context", cross)
-    near, keys, all_values = gather(queries, out_grad, key_rows, values, ranks)
-    slot = (x * 2 + core).astype(jnp.int32)
-    zero, one = jnp.int32(0), jnp.int32(1)
-    own_rows, near_rows, dk, dv, pair_count = attend(
-        (queries, out_grad, near, near), jnp.stack([slot, slot, zero, one]), keys, all_values, lengths,
-        block_owner=block_owner,
+    chips = [(a, b, c) for a in range(2) for b in range(YS) for c in range(2)]
+    same = [(rank_of(a, b, c), rank_of(1 - a, b, c)) for a, b, c in chips]
+    cross = [(rank_of(a, b, c), rank_of(1 - a, b, 1 - c)) for a, b, c in chips]
+    rows, keys, all_values = gather(queries, out_grad, key_rows, values, ranks)
+    slot = (x * 2 + core).astype(jnp.int32).reshape(1)
+    own, near, far_same, far_cross, dk, dv, pair_count = attend(
+        queries, out_grad, rows, slot, keys, all_values, lengths, block_owner
     )
-    same_rows, cross_rows, dk, dv = attend(
-        (far_same, far_same, far_cross, far_cross), jnp.stack([zero, one, zero, one]), keys, all_values, lengths,
-        old=(dk, dv),
-    )
-    same_rows = lax.ppermute(same_rows, "context", same)
-    cross_rows = lax.ppermute(cross_rows, "context", cross)
-    near_rows, key_grad, value_grad = scatter(dk, dv, near_rows, ranks)
-    out, query_grad = place_columns((own_rows, near_rows, same_rows, cross_rows))
+    far_same = lax.ppermute(far_same, "context", same)
+    far_cross = lax.ppermute(far_cross, "context", cross)
+    near, key_grad, value_grad = scatter(dk, dv, near, ranks)
+    out, query_grad = place_columns((own, near, far_same, far_cross))
     return out, query_grad, key_grad, value_grad, pair_count
 
 

time: 210 us -> 132 us (0.63)
  the two profiles are of different devices: /device:TPU:32 before, /device:TPU:21 now
where the time goes in v3:
time: 132 us
  Pallas kernels  128 us (97%)
  local copies, waits for them, and re-layouts  2.26 us (2%)
  starting transfers between devices  1.38 us (1%)
    pallas_call x1, Pallas kernels, attend(): pl.pallas_call(attend_kernel, grid_spec=pltpu.PrefetchScalarGridSpec(num_...  60.2 us
    pallas_call x1, Pallas kernels, gather(): pl.pallas_call(gather_kernel, in_specs=[any_spec] * 4, out_specs=[any_spe...  32.4 us
    pallas_call x1, Pallas kernels, scatter(): pl.pallas_call(scatter_kernel, in_specs=[any_spec] * 3, out_specs=[any_sp...  31.3 us
    pallas_call x1, Pallas kernels, place_columns(): pl.pallas_call(place_kernel, grid=(shard // block,), in_specs=[pl.BlockSp...  3.9 us
  transfers between devices with their start and end apart: 2, of which 0 were waited for; matrix products, arithmetic and copies ran while one was open for 0% of the time, Pallas kernels for 24%

profile of v3, /device:TPU:21, one launch (start us, length us, event | category | flops | bytes accessed | tf_op | source)
XLA Modules:
  0.0 132.2 jit_solution(15687846086129450587)
XLA Ops:
  0.7 32.4 %gather.1 = (bf16[1536,512]{1,0:T(8,128)(2,1)}, bf16[8192,128]{1,0:T(8,128)(2,1)}, bf16[8192,128]{1,0:T(8,128)(2,1)}) custom-call(bf16[512,1024]{1,0:T(8,128)(2,1)} %q0_ref.1, bf16[512,1024]{1,0:T(8,128)(2,1)} %g0_ref.1, bf16[512,128]{1,0:T(8,128)(2,1)} %k_ref.1, bf16[512,128]{1,0:T(8,128)(2,1)} %v_ref.1), custom_call_target="tpu_custom_call" | custom-call | tf_op jit(solution)/shard_map/gather/pallas_call | solution.py:163
  33.1 60.2 %attend.1 = (bf16[512,512]{1,0:T(8,128)(2,1)}, bf16[512,512]{1,0:T(8,128)(2,1)}, bf16[512,512]{1,0:T(8,128)(2,1)}, bf16[512,512]{1,0:T(8,128)(2,1)}, bf16[8192,1...) custom-call(s32[16]{0:T(128)} %len_ref.1, s32[1]{0:T(128)} %bitcast.slot_ref, s32[1,128]{1,0:T(1,128)} %bitcast.2, ...), custom_call_target="tpu_custom_call" | custom-call | flops 20000000000 | bytes 20000000 | tf_op jit(solution)/shard_map/attend/pallas_call | solution.py:406
  93.3 1.0 collective-permute-start
  94.3 0.4 collective-permute-start.1
  94.7 31.3 %scatter.1 = (bf16[512,512]{1,0:T(8,128)(2,1)}, bf16[512,128]{1,0:T(8,128)(2,1)}, bf16[512,128]{1,0:T(8,128)(2,1)}) custom-call(bf16[8192,128]{1,0:T(8,128)(2,1)} %get-tuple-element.24.dk_ref, bf16[8192,128]{1,0:T(8,128)(2,1)} %get-tuple-element.25.dv_ref, bf16[512,512]{1,0:T(8,128)(2,1)} %get-tuple-element.26.rows_ref), custom_call_target="tpu_custom_call" | custom-call | flops 20000000 | bytes 20000000 | tf_op jit(solution)/shard_map/scatter/pallas_call | solution.py:543
  126.0 0.0 copy-start.3
  126.0 0.0 copy-start.2
  126.0 0.0 collective-permute-done.c_ref
  126.0 0.0 copy-start
  126.0 0.0 collective-permute-done.1.d_ref
  126.0 0.0 copy-start.1
  126.1 0.8 copy-done
  126.8 0.2 copy-done.1
  127.0 3.9 %place.1 = (bf16[512,1024]{1,0:T(8,128)(2,1)}, bf16[512,1024]{1,0:T(8,128)(2,1)}) custom-call(bf16[512,512]{1,0:T(8,128)(2,1)} %get-tuple-element.23.a_ref, bf16[512,512]{1,0:T(8,128)(2,1)} %get-tuple-element.27.b_ref, bf16[512,512]{1,0:T(8,128)(2,1)} %copy-done, bf16[512,512]{1,0:T(8,128)(2,1)} %copy-done.1), custom_call_target="tpu_custom_call" | custom-call | tf_op jit(solution)/shard_map/place/pallas_call | solution.py:583
  130.9 0.0 copy-done.3
  130.9 0.7 copy.13
  131.5 0.0 copy-done.2
  131.6 0.7 copy.14
Async XLA Ops:
  93.3 32.7 %collective-permute-start = (bf16[512,512]{1,0:T(8,128)(2,1)}, bf16[512,512]{1,0:T(8,128)(2,1)S(1)}, u32[]{:S(2)}, u32[]{:S(2)}) collective-permute-start(bf16[512,512]{1,0:T(8,128)(2,1)} %get-tuple-element.28), channel_id=1, source_target_pairs={{0,8},{1,9},{2,10},{3,11},{4,12},{5,13},{6,14},{7,15},{8,0},{9,1},... | collective-permute-start | bytes 1572872 | tf_op jit(solution)/shard_map/ppermute | solution.py:605
  94.3 31.7 %collective-permute-start.1 = (bf16[512,512]{1,0:T(8,128)(2,1)}, bf16[512,512]{1,0:T(8,128)(2,1)S(1)}, u32[]{:S(2)}, u32[]{:S(2)}) collective-permute-start(bf16[512,512]{1,0:T(8,128)(2,1)} %get-tuple-element.29), channel_id=1, source_target_pairs={{0,9},{1,8},{2,11},{3,10},{4,13},{5,12},{6,15},{7,14},{8,1},{9,0},... | collective-permute-start | bytes 1572872 | tf_op jit(solution)/shard_map/ppermute | solution.py:606
  126.0 4.9 %copy-start.3 = (bf16[512,128]{1,0:T(8,128)(2,1)S(1)}, bf16[512,128]{1,0:T(8,128)(2,1)}, u32[]{:S(2)}) copy-start(bf16[512,128]{1,0:T(8,128)(2,1)} %get-tuple-element.42) | copy-start | bytes 393220
  126.0 5.5 %copy-start.2 = (bf16[512,128]{1,0:T(8,128)(2,1)S(1)}, bf16[512,128]{1,0:T(8,128)(2,1)}, u32[]{:S(2)}) copy-start(bf16[512,128]{1,0:T(8,128)(2,1)} %get-tuple-element.43) | copy-start | bytes 393220
  126.0 0.8 copy-start
  126.0 0.9 copy-start.1

commit v4 on v3

--- a/solution.py
+++ b/solution.py
@@ -12,7 +12,8 @@
 MESH = pl.DeviceIdType.MESH
 YS = 4
 HD = 128
-HEADS_HERE = 2
+NEAR = 3
+FAR = 1
 GROUP = 4
 TILE = 256
 SPAN = 4
@@ -62,14 +63,26 @@
     return pl.ds(pl.multiple_of(begin, count), count)
 
 
+def head_cols(d, core):
+    heads = NEAR if d < 2 else FAR
+    at = core * NEAR * HD if d < 2 else 2 * NEAR * HD + core * FAR * HD
+    return pl.ds(pl.multiple_of(at, HD), heads * HD)
+
+
+def rows_from(near_ref, far_ref, d, a):
+    if d < 2:
+        return near_ref.at[:, pl.ds(a * NEAR * HD, NEAR * HD)]
+    shard = near_ref.shape[0]
+    return far_ref.at[pl.ds((d - 2) * shard, shard), pl.ds(a * FAR * HD, FAR * HD)]
+
+
 def gather_kernel(
-    q_ref, g_ref, k_ref, v_ref, rows_ref, ka_ref, va_ref,
+    q_ref, g_ref, k_ref, v_ref, near_ref, far_ref, ka_ref, va_ref,
     own_sem, kv_send, kv_recv, core_send, core_recv, row_send, row_recv,
 ):
     x, y, core = place()
     shard = k_ref.shape[0]
     half = shard // 2
-    width = q_ref.shape[1] // GROUP
     up, down, far = (y + 1) % YS, (y + YS - 1) % YS, (y + 2) % YS
     x_rank = rank_of(1 - x, y, core)
     core_rank = rank_of(x, y, 1 - core)
@@ -100,9 +113,8 @@
     for a, src in enumerate((q_ref, g_ref)):
         for d in range(1, GROUP):
             tx, tc = (x + d // 2) % 2, (core + d % 2) % 2
-            cols = pl.ds(pl.multiple_of((tx * 2 + tc) * width, width), width)
             send(
-                src.at[:, cols], rows_ref.at[pl.ds((d - 1) * shard, shard), pl.ds(a * width, width)],
+                src.at[:, head_cols(d, tc)], rows_from(near_ref, far_ref, d, a),
                 row_send.at[a, d - 1], row_recv.at[a, d - 1], rank_of(tx, y, tc),
             )
 
@@ -147,7 +159,7 @@
                 landed(dst.at[half_rows(sx, far, oc, h)], core_recv.at[a, 5 + n + h])
     for a in range(2):
         for d in range(1, GROUP):
-            landed(rows_ref.at[pl.ds((d - 1) * shard, shard), pl.ds(a * width, width)], row_recv.at[a, d - 1])
+            landed(rows_from(near_ref, far_ref, d, a), row_recv.at[a, d - 1])
     for copy in own:
         copy.wait()
     for copy in started:
@@ -155,17 +167,17 @@
 
 
 def gather(queries, out_grad, keys, values, ranks):
-    shard, feature = queries.shape
-    width = feature // GROUP
+    shard = queries.shape[0]
     bf16 = jnp.bfloat16
     any_spec = pl.BlockSpec(memory_space=pl.ANY)
     dma = pltpu.SemaphoreType.DMA
     return pl.pallas_call(
         gather_kernel,
         in_specs=[any_spec] * 4,
-        out_specs=[any_spec] * 3,
+        out_specs=[any_spec] * 4,
         out_shape=[
-            jax.ShapeDtypeStruct(((GROUP - 1) * shard, 2 * width), bf16),
+            jax.ShapeDtypeStruct((shard, 2 * NEAR * HD), bf16),
+            jax.ShapeDtypeStruct((2 * shard, 2 * FAR * HD), bf16),
             jax.ShapeDtypeStruct((ranks * shard, HD), bf16),
             jax.ShapeDtypeStruct((ranks * shard, HD), bf16),
         ],
@@ -181,21 +193,149 @@
     return jnp.dot(a, b, preferred_element_type=jnp.float32)
 
 
+def attend_block(
+    heads, block, first, len_ref, inputs, outputs, k_ref, v_ref, kt_ref, vt_ref, dka_ref, dva_ref,
+    p_ref, qt_ref, gt_ref, qn_ref, gn_ref, ds_ref, acc_ref,
+):
+    f32, bf16 = jnp.float32, jnp.bfloat16
+    cols = block * heads
+    docs = len_ref.shape[0]
+    scale = 1.0 / math.sqrt(HD)
+    scale2 = scale * math.log2(math.e)
+    row_pos = first + lax.rem(lax.broadcasted_iota(jnp.int32, (1, cols), 1), block)
+    row_start = jnp.zeros((1, cols), jnp.int32)
+    first_start, last_start, end = jnp.int32(0), jnp.int32(0), jnp.int32(0)
+    for d in range(docs):
+        end = end + len_ref[d]
+        row_start = jnp.where(row_pos >= end, end, row_start)
+        first_start = jnp.where(first >= end, end, first_start)
+        last_start = jnp.where(first + block - 1 >= end, end, last_start)
+    low = lax.div(first_start, TILE)
+    high = lax.div(first + block - 1, TILE) + 1
+
+    own_keys = kt_ref[:, rows_at(first, block)].astype(f32)
+    shift = []
+    for h in range(heads):
+        for chosen, q_ref, g_ref in inputs:
+
+            @pl.when(chosen)
+            def _(h=h, q_ref=q_ref, g_ref=g_ref):
+                qt_ref[:, h * block : (h + 1) * block] = q_ref[:, h * HD : (h + 1) * HD].T
+                gt_ref[:, h * block : (h + 1) * block] = g_ref[:, h * HD : (h + 1) * HD].T
+
+        q_t = qt_ref[:, h * block : (h + 1) * block]
+        shift.append(jnp.sum(q_t.astype(f32) * own_keys, axis=0, keepdims=True) * scale2)
+    shift = jnp.concatenate(shift, axis=1)
+
+    def keep(result, at):
+        for chosen, r_ref in outputs:
+
+            @pl.when(chosen)
+            def _(r_ref=r_ref):
+                for h in range(heads):
+                    cut = result[h * block : (h + 1) * block, :]
+                    r_ref[:, (at + h) * HD : (at + h + 1) * HD] = cut
+
+    def key_rows(t, count):
+        return pl.ds(pl.multiple_of(t * TILE, TILE), count)
+
+    def kept_rows(t, count):
+        return pl.ds(pl.multiple_of((t - low) * TILE, TILE), count)
+
+    def sweep(piece):
+        count = high - low
+        groups = lax.div(count, SPAN)
+
+        def one(g, carry):
+            piece(low + g * SPAN, SPAN * TILE, False)
+            return carry
+
+        lax.fori_loop(0, groups, one, 0)
+        at = low + groups * SPAN
+        size = SPAN // 2
+        while size:
+            has = lax.rem(lax.div(count, size), 2)
+
+            @pl.when(has == 1)
+            def _(at=at, size=size):
+                piece(at, size * TILE, True)
+
+            at = at + has * size
+            size //= 2
+
+    def forward(shift):
+        acc_ref[...] = jnp.zeros(acc_ref.shape, f32)
+
+        def piece(t, rows, last):
+            def run(mask):
+                acc = None
+                part = min(rows, PASS)
+                for i in range(0, rows, part):
+                    tile = t + i // TILE
+                    s = dot(k_ref[key_rows(tile, part), :], qt_ref[...]) * scale2 - shift
+                    if mask:
+                        pos = t * TILE + i + lax.broadcasted_iota(jnp.int32, s.shape, 0)
+                        s = jnp.where((pos >= row_start) & (pos <= row_pos), s, NEG_FILL)
+                    p_ref[kept_rows(tile, part), :] = jnp.exp2(s).astype(bf16)
+                    term = dot(vt_ref[:, key_rows(tile, part)], p_ref[kept_rows(tile, part), :])
+                    acc = term if acc is None else acc + term
+                acc_ref[...] += acc
+
+            if last:
+                run(True)
+            else:
+                edge = (t * TILE < last_start) | (t * TILE + rows - 1 > first)
+                pl.when(edge)(lambda: run(True))
+                pl.when(jnp.logical_not(edge))(lambda: run(False))
+
+        sweep(piece)
+
+    forward(shift)
+
+    @pl.when(jnp.logical_not(jnp.max(acc_ref[HD : HD + 1, :]) < LARGE))
+    def _():
+        def peak_pass(t, peak):
+            s = dot(k_ref[key_rows(t, TILE), :], qt_ref[...]) * scale2
+            pos = t * TILE + lax.broadcasted_iota(jnp.int32, s.shape, 0)
+            s = jnp.where((pos >= row_start) & (pos <= row_pos), s, NEG_FILL)
+            return jnp.maximum(peak, jnp.max(s.reshape(TILE // 8, 8, cols), axis=0))
+
+        peak = lax.fori_loop(low, high, peak_pass, jnp.full((8, cols), NEG_FILL, f32))
+        forward(jnp.max(peak, axis=0, keepdims=True))
+
+    inverse = 1.0 / acc_ref[HD : HD + 1, :]
+    out = (acc_ref[0:HD, :] * inverse).astype(bf16)
+    grad_t = gt_ref[...].astype(f32)
+    grad_dot = jnp.sum(out.astype(f32) * grad_t, axis=0, keepdims=True)
+    gn_ref[...] = (grad_t * inverse).astype(bf16).T
+    qn_ref[...] = (qt_ref[...].astype(f32) * inverse).astype(bf16).T
+    keep(out.T, 0)
+    acc_ref[0:HD, :] = jnp.zeros((HD, cols), f32)
+
+    def backward(t, rows, last):
+        keys, kept = key_rows(t, rows), kept_rows(t, rows)
+        grad_p = dot(v_ref[keys, :], gt_ref[...])
+        ds_ref[0:rows, :] = (p_ref[kept, :].astype(f32) * (grad_p - grad_dot)).astype(bf16)
+        dva_ref[keys, :] += dot(p_ref[kept, :], gn_ref[...])
+        dka_ref[keys, :] += dot(ds_ref[0:rows, :], qn_ref[...])
+        acc_ref[0:HD, :] += dot(kt_ref[:, keys], ds_ref[0:rows, :])
+
+    sweep(backward)
+    query_grad = (acc_ref[0:HD, :] * (inverse * scale)).astype(bf16).T
+    keep(query_grad, heads)
+
+
 def attend_kernel(
-    len_ref, slot_ref, owner_ref, q0_ref, g0_ref, q1_ref, g1_ref, k_ref, v_ref,
+    len_ref, core_ref, owner_ref, q0_ref, g0_ref, q1_ref, g1_ref, q2_ref, g2_ref, k_ref, v_ref,
     r0_ref, r1_ref, r2_ref, r3_ref, dk_ref, dv_ref, pair_ref,
     kt_ref, vt_ref, p_ref, qt_ref, gt_ref, qn_ref, gn_ref, dka_ref, dva_ref, ds_ref, acc_ref,
 ):
     blk = pl.program_id(0)
-    q_refs, g_refs, r_refs = (q0_ref, q1_ref), (g0_ref, g1_ref), (r0_ref, r1_ref, r2_ref, r3_ref)
-    block, width = q0_ref.shape
-    heads = width // HD
-    cols = block * heads
+    block = q0_ref.shape[0]
     tokens = k_ref.shape[0]
     docs = len_ref.shape[0]
     f32, bf16 = jnp.float32, jnp.bfloat16
     scale = 1.0 / math.sqrt(HD)
-    scale2 = scale * math.log2(math.e)
     x, y, core = place()
     per_chip = tokens // (2 * YS)
     per_core = pl.num_programs(0) // GROUP
@@ -239,127 +379,27 @@
     chip = lax.rem(x + lax.div(part, 2), 2) * YS + y
     row_core = lax.rem(core + part, 2)
     first = chip * per_chip + row_core * (per_chip // 2) + lax.rem(blk, per_core) * block
-    row_pos = first + lax.rem(lax.broadcasted_iota(jnp.int32, (1, cols), 1), block)
-    row_start = jnp.zeros((1, cols), jnp.int32)
-    first_start, last_start, end = jnp.int32(0), jnp.int32(0), jnp.int32(0)
-    for d in range(docs):
-        end = end + len_ref[d]
-        row_start = jnp.where(row_pos >= end, end, row_start)
-        first_start = jnp.where(first >= end, end, first_start)
-        last_start = jnp.where(first + block - 1 >= end, end, last_start)
-    low = lax.div(first_start, TILE)
-    high = lax.div(first + block - 1, TILE) + 1
-
-    own_keys = kt_ref[:, rows_at(first, block)].astype(f32)
-    shift = []
-    for h in range(heads):
-        for n in range(2):
-
-            @pl.when((part > 0) == bool(n))
-            def _(n=n, h=h):
-                qt_ref[:, h * block : (h + 1) * block] = q_refs[n][:, h * HD : (h + 1) * HD].T
-                gt_ref[:, h * block : (h + 1) * block] = g_refs[n][:, h * HD : (h + 1) * HD].T
-
-        q_t = qt_ref[:, h * block : (h + 1) * block]
-        shift.append(jnp.sum(q_t.astype(f32) * own_keys, axis=0, keepdims=True) * scale2)
-    shift = jnp.concatenate(shift, axis=1)
-
-    def keep(result, at):
-        for n in range(GROUP):
-
-            @pl.when(part == n)
-            def _(n=n):
-                for h in range(heads):
-                    cut = result[h * block : (h + 1) * block, :]
-                    r_refs[n][:, (at + h) * HD : (at + h + 1) * HD] = cut
-
-    def key_rows(t, count):
-        return pl.ds(pl.multiple_of(t * TILE, TILE), count)
-
-    def kept_rows(t, count):
-        return pl.ds(pl.multiple_of((t - low) * TILE, TILE), count)
-
-    def sweep(piece):
-        count = high - low
-        groups = lax.div(count, SPAN)
-
-        def one(g, carry):
-            piece(low + g * SPAN, SPAN * TILE, False)
-            return carry
-
-        lax.fori_loop(0, groups, one, 0)
-        at = low + groups * SPAN
-        size = SPAN // 2
-        while size:
-            has = lax.rem(lax.div(count, size), 2)
-
-            @pl.when(has == 1)
-            def _(at=at, size=size):
-                piece(at, size * TILE, True)
-
-            at = at + has * size
-            size //= 2
-
-    def forward(shift):
-        acc_ref[...] = jnp.zeros(acc_ref.shape, f32)
-
-        def piece(t, rows, last):
-            def run(mask):
-                acc = None
-                part = min(rows, PASS)
-                for i in range(0, rows, part):
-                    tile = t + i // TILE
-                    s = dot(k_ref[key_rows(tile, part), :], qt_ref[...]) * scale2 - shift
-                    if mask:
-                        pos = t * TILE + i + lax.broadcasted_iota(jnp.int32, s.shape, 0)
-                        s = jnp.where((pos >= row_start) & (pos <= row_pos), s, NEG_FILL)
-                    p_ref[kept_rows(tile, part), :] = jnp.exp2(s).astype(bf16)
-                    term = dot(vt_ref[:, key_rows(tile, part)], p_ref[kept_rows(tile, part), :])
-                    acc = term if acc is None else acc + term
-                acc_ref[...] += acc
-
-            if last:
-                run(True)
-            else:
-                edge = (t * TILE < last_start) | (t * TILE + rows - 1 > first)
-                pl.when(edge)(lambda: run(True))
-                pl.when(jnp.logical_not(edge))(lambda: run(False))
-
-        sweep(piece)
-
-    forward(shift)
-
-    @pl.when(jnp.logical_not(jnp.max(acc_ref[HD : HD + 1, :]) < LARGE))
+
+    def work(heads, inputs, outputs):
+        cols = block * heads
+        scratch = (
+            p_ref.at[:, 0:cols], qt_ref.at[:, 0:cols], gt_ref.at[:, 0:cols], qn_ref.at[0:cols], gn_ref.at[0:cols],
+            ds_ref.at[:, 0:cols], acc_ref.at[:, 0:cols],
+        )
+        attend_block(
+            heads, block, first, len_ref, inputs, outputs, k_ref, v_ref, kt_ref, vt_ref, dka_ref, dva_ref, *scratch
+        )
+
+    @pl.when(part < 2)
     def _():
-        def peak_pass(t, peak):
-            s = dot(k_ref[key_rows(t, TILE), :], qt_ref[...]) * scale2
-            pos = t * TILE + lax.broadcasted_iota(jnp.int32, s.shape, 0)
-            s = jnp.where((pos >= row_start) & (pos <= row_pos), s, NEG_FILL)
-            return jnp.maximum(peak, jnp.max(s.reshape(TILE // 8, 8, cols), axis=0))
-
-        peak = lax.fori_loop(low, high, peak_pass, jnp.full((8, cols), NEG_FILL, f32))
-        forward(jnp.max(peak, axis=0, keepdims=True))
-
-    inverse = 1.0 / acc_ref[HD : HD + 1, :]
-    out = (acc_ref[0:HD, :] * inverse).astype(bf16)
-    grad_t = gt_ref[...].astype(f32)
-    grad_dot = jnp.sum(out.astype(f32) * grad_t, axis=0, keepdims=True)
-    gn_ref[...] = (grad_t * inverse).astype(bf16).T
-    qn_ref[...] = (qt_ref[...].astype(f32) * inverse).astype(bf16).T
-    keep(out.T, 0)
-    acc_ref[0:HD, :] = jnp.zeros((HD, cols), f32)
-
-    def backward(t, rows, last):
-        keys, kept = key_rows(t, rows), kept_rows(t, rows)
-        grad_p = dot(v_ref[keys, :], gt_ref[...])
-        ds_ref[0:rows, :] = (p_ref[kept, :].astype(f32) * (grad_p - grad_dot)).astype(bf16)
-        dva_ref[keys, :] += dot(p_ref[kept, :], gn_ref[...])
-        dka_ref[keys, :] += dot(ds_ref[0:rows, :], qn_ref[...])
-        acc_ref[0:HD, :] += dot(kt_ref[:, keys], ds_ref[0:rows, :])
-
-    sweep(backward)
-    query_grad = (acc_ref[0:HD, :] * (inverse * scale)).astype(bf16).T
-    keep(query_grad, heads)
+        work(
+            NEAR, ((part == 0, q0_ref, g0_ref), (part == 1, q1_ref, g1_ref)),
+            ((part == 0, r0_ref), (part == 1, r1_ref)),
+        )
+
+    @pl.when(part >= 2)
+    def _():
+        work(FAR, ((part >= 2, q2_ref, g2_ref),), ((part == 2, r2_ref), (part == 3, r3_ref)))
 
     @pl.when(blk == pl.num_programs(0) - 1)
     def _():
@@ -383,22 +423,27 @@
         lax.fori_loop(0, tokens // PASS, finish, 0)
 
 
-def attend(queries, out_grad, rows, slot, keys, values, lengths, block_owner):
+def attend(queries, out_grad, near, far, core, keys, values, lengths, block_owner):
     tokens = keys.shape[0]
     shard = queries.shape[0]
     per_core = shard // QBLOCK
-    width = HEADS_HERE * HD
     span = ((DOC_MAX + QBLOCK + TILE - 2) // TILE + 1) * TILE
-    qcols = QBLOCK * HEADS_HERE
-
-    def own_spec():
-        return pl.BlockSpec((QBLOCK, width), lambda i, _, slot: (jnp.minimum(i, per_core - 1), slot[0]))
-
-    def other_spec(col):
-        return pl.BlockSpec((QBLOCK, width), lambda i, *_: (jnp.maximum(i - per_core, 0), col))
+    qcols = QBLOCK * NEAR
+
+    def step(i, n):
+        return jnp.clip(i - n * per_core, 0, per_core - 1)
+
+    own_spec = pl.BlockSpec((QBLOCK, NEAR * HD), lambda i, _, core: (step(i, 0), core[0]))
+
+    def near_spec(col):
+        return pl.BlockSpec((QBLOCK, NEAR * HD), lambda i, *_: (step(i, 1), col))
+
+    def far_spec(col):
+        return pl.BlockSpec((QBLOCK, FAR * HD), lambda i, *_: (jnp.maximum(i - 2 * per_core, 0), col))
 
     def result_spec(n):
-        return pl.BlockSpec((QBLOCK, 2 * width), lambda i, *_: (jnp.clip(i - n * per_core, 0, per_core - 1), 0))
+        heads = NEAR if n < 2 else FAR
+        return pl.BlockSpec((QBLOCK, 2 * heads * HD), lambda i, *_: (step(i, n), 0))
 
     full_spec = pl.BlockSpec((tokens, HD), lambda i, *_: (0, 0))
     bf16, f32 = jnp.bfloat16, jnp.float32
@@ -409,7 +454,8 @@
             num_scalar_prefetch=2,
             grid=(GROUP * per_core,),
             in_specs=[
-                owner_spec, own_spec(), own_spec(), other_spec(0), other_spec(1), full_spec, full_spec,
+                owner_spec, own_spec, own_spec, near_spec(0), near_spec(1), far_spec(0), far_spec(1),
+                full_spec, full_spec,
             ],
             out_specs=[result_spec(n) for n in range(GROUP)]
             + [full_spec, full_spec, pl.BlockSpec(memory_space=pltpu.SMEM)],
@@ -427,13 +473,14 @@
                 pltpu.VMEM((HD + ONES, qcols), f32),
             ],
         ),
-        out_shape=[jax.ShapeDtypeStruct((shard, 2 * width), bf16)] * GROUP
+        out_shape=[jax.ShapeDtypeStruct((shard, 2 * NEAR * HD), bf16)] * 2
+        + [jax.ShapeDtypeStruct((shard, 2 * FAR * HD), bf16)] * 2
         + [jax.ShapeDtypeStruct((tokens, HD), bf16)] * 2
         + [jax.ShapeDtypeStruct((1,), f32)],
         cost_estimate=pl.CostEstimate(flops=2 * 10**10, bytes_accessed=2 * 10**7, transcendentals=5 * 10**6),
         compiler_params=pltpu.CompilerParams(vmem_limit_bytes=62 * 2**20),
         name="attend",
-    )(lengths, slot, block_owner.reshape(1, -1), queries, out_grad, rows, rows, keys, values)
+    )(lengths, core, block_owner.reshape(1, -1), queries, out_grad, near, near, far, far, keys, values)
 
 
 def scatter_kernel(
@@ -566,46 +613,53 @@
     )(key_terms, value_terms, rows)
 
 
-def place_kernel(a_ref, b_ref, c_ref, d_ref, o_ref, q_ref):
-    x, _, core = place()
-    width = a_ref.shape[1] // 2
+def place_kernel(a_ref, b_ref, c_ref, d_ref, k_ref, v_ref, o_ref, q_ref, key_ref, value_ref):
+    _, _, core = place()
     for d, ref in enumerate((a_ref, b_ref, c_ref, d_ref)):
-        slot = ((x + d // 2) % 2) * 2 + (core + d % 2) % 2
-        cols = pl.ds(pl.multiple_of(slot * width, width), width)
+        cols = head_cols(d, (core + d % 2) % 2)
+        width = ref.shape[1] // 2
         o_ref[:, cols] = ref[:, :width]
         q_ref[:, cols] = ref[:, width:]
-
-
-def place_columns(pieces):
-    shard, width = pieces[0].shape
-    block = shard // 4
-    shape = jax.ShapeDtypeStruct((shard, width * 2), jnp.bfloat16)
+    key_ref[...] = k_ref[...]
+    value_ref[...] = v_ref[...]
+
+
+def place_columns(pieces, key_grad, value_grad):
+    shard = key_grad.shape[0]
+    block = shard // 2
+    feature = sum(piece.shape[1] for piece in pieces) // 2
+
+    def spec(width):
+        return pl.BlockSpec((block, width), lambda i: (i, 0))
+
     return pl.pallas_call(
         place_kernel,
         grid=(shard // block,),
-        in_specs=[pl.BlockSpec((block, width), lambda i: (i, 0))] * GROUP,
-        out_specs=[pl.BlockSpec((block, width * 2), lambda i: (i, 0))] * 2,
-        out_shape=[shape, shape],
+        in_specs=[spec(piece.shape[1]) for piece in pieces] + [spec(HD)] * 2,
+        out_specs=[spec(feature)] * 2 + [spec(HD)] * 2,
+        out_shape=[jax.ShapeDtypeStruct((shard, feature), jnp.bfloat16)] * 2
+        + [jax.ShapeDtypeStruct((shard, HD), jnp.bfloat16)] * 2,
         compiler_params=pltpu.CompilerParams(vmem_limit_bytes=62 * 2**20),
         name="place",
-    )(*pieces)
+    )(*pieces, key_grad, value_grad)
 
 
 def body(queries, key_rows, values, out_grad, lengths, block_owner):
     ranks = lax.axis_size("context")
-    x, _, core = place()
+    _, _, core = place()
     chips = [(a, b, c) for a in range(2) for b in range(YS) for c in range(2)]
     same = [(rank_of(a, b, c), rank_of(1 - a, b, c)) for a, b, c in chips]
     cross = [(rank_of(a, b, c), rank_of(1 - a, b, 1 - c)) for a, b, c in chips]
-    rows, keys, all_values = gather(queries, out_grad, key_rows, values, ranks)
-    slot = (x * 2 + core).astype(jnp.int32).reshape(1)
+    near, far, keys, all_values = gather(queries, out_grad, key_rows, values, ranks)
     own, near, far_same, far_cross, dk, dv, pair_count = attend(
-        queries, out_grad, rows, slot, keys, all_values, lengths, block_owner
+        queries, out_grad, near, far, core.astype(jnp.int32).reshape(1), keys, all_values, lengths, block_owner
     )
     far_same = lax.ppermute(far_same, "context", same)
     far_cross = lax.ppermute(far_cross, "context", cross)
     near, key_grad, value_grad = scatter(dk, dv, near, ranks)
-    out, query_grad = place_columns((own, near, far_same, far_cross))
+    out, query_grad, key_grad, value_grad = place_columns(
+        (own, near, far_same, far_cross), key_grad, value_grad
+    )
     return out, query_grad, key_grad, value_grad, pair_count
 
 

time: 132 us -> 125 us (0.947)
  the two profiles are of different devices: /device:TPU:21 before, /device:TPU:96 now
where the time goes in v4:
time: 125 us
  Pallas kernels  116 us (93%)
  starting transfers between devices  7.91 us (6%)
    pallas_call x1, Pallas kernels, scatter(): pl.pallas_call(scatter_kernel, in_specs=[any_spec] * 3, out_specs=[any_sp...  56.1 us
    pallas_call x1, Pallas kernels, attend(): pl.pallas_call(attend_kernel, grid_spec=pltpu.PrefetchScalarGridSpec(num_...  32.1 us
    pallas_call x1, Pallas kernels, gather(): pl.pallas_call(gather_kernel, in_specs=[any_spec] * 4, out_specs=[any_spe...  25 us
    ppermute x1, starting transfers between devices, body(): far_same = lax.ppermute(far_same, 'context', same)  7.76 us
    pallas_call x1, Pallas kernels, place_columns(): pl.pallas_call(place_kernel, grid=(shard // block,), in_specs=[spec(piece...  2.78 us
  transfers between devices with their start and end apart: 2, of which 0 were waited for; matrix products, arithmetic and copies ran while one was open for 0% of the time, Pallas kernels for 45%

profile of v4, /device:TPU:96, one launch (start us, length us, event | category | flops | bytes accessed | tf_op | source)
XLA Modules:
  0.0 125.3 jit_solution(15570243622561550267)
XLA Ops:
  0.6 25.0 %gather.1 = (bf16[512,768]{1,0:T(8,128)(2,1)}, bf16[1024,256]{1,0:T(8,128)(2,1)}, bf16[8192,128]{1,0:T(8,128)(2,1)}, bf16[8192,128]{1,0:T(8,128)(2,1)}) custom-call(bf16[512,1024]{1,0:T(8,128)(2,1)} %q0_ref.1, bf16[512,1024]{1,0:T(8,128)(2,1)} %g0_ref.1, bf16[512,128]{1,0:T(8,128)(2,1)} %k_ref.1, bf16[512,128]{1,0:T(8,128)(2,1)} %v_ref.1), custom_call_target="tpu_custom_call" | custom-call | tf_op jit(solution)/shard_map/gather/pallas_call | solution.py:174
  25.6 32.1 %attend.1 = (bf16[512,768]{1,0:T(8,128)(2,1)}, bf16[512,768]{1,0:T(8,128)(2,1)}, bf16[512,256]{1,0:T(8,128)(2,1)}, bf16[512,256]{1,0:T(8,128)(2,1)}, bf16[8192,1...) custom-call(s32[16]{0:T(128)} %len_ref.1, s32[1]{0:T(128)} %bitcast.core_ref, s32[1,128]{1,0:T(1,128)} %bitcast.2, ...), custom_call_target="tpu_custom_call" | custom-call | flops 20000000000 | bytes 20000000 | tf_op jit(solution)/shard_map/attend/pallas_call | solution.py:451
  57.7 7.8 %collective-permute-start = (bf16[512,256]{1,0:T(8,128)(2,1)}, bf16[512,256]{1,0:T(8,128)(2,1)S(1)}, u32[]{:S(2)}, u32[]{:S(2)}) collective-permute-start(bf16[512,256]{1,0:T(8,128)(2,1)} %get-tuple-element.32), channel_id=1, source_target_pairs={{0,8},{1,9},{2,10},{3,11},{4,12},{5,13},{6,14},{7,15},{8,0},{9,1},... | collective-permute-start | bytes 786440 | tf_op jit(solution)/shard_map/ppermute | solution.py:657
  65.4 0.1 collective-permute-start.1
  65.6 56.1 %scatter.1 = (bf16[512,768]{1,0:T(8,128)(2,1)}, bf16[512,128]{1,0:T(8,128)(2,1)}, bf16[512,128]{1,0:T(8,128)(2,1)}) custom-call(bf16[8192,128]{1,0:T(8,128)(2,1)} %get-tuple-element.28.dk_ref, bf16[8192,128]{1,0:T(8,128)(2,1)} %get-tuple-element.29.dv_ref, bf16[512,768]{1,0:T(8,128)(2,1)} %get-tuple-element.30.rows_ref), custom_call_target="tpu_custom_call" | custom-call | flops 20000000 | bytes 20000000 | tf_op jit(solution)/shard_map/scatter/pallas_call | solution.py:590
  121.7 0.0 collective-permute-done.c_ref
  121.7 0.0 copy-start
  121.7 0.0 collective-permute-done.1.d_ref
  121.7 0.0 copy-start.1
  121.7 0.7 copy-done
  122.4 0.1 copy-done.1
  122.6 2.8 %place.1 = (bf16[512,1024]{1,0:T(8,128)(2,1)}, bf16[512,1024]{1,0:T(8,128)(2,1)}, bf16[512,128]{1,0:T(8,128)(2,1)}, bf16[512,128]{1,0:T(8,128)(2,1)}) custom-call(bf16[512,768]{1,0:T(8,128)(2,1)} %get-tuple-element.27.a_ref, bf16[512,768]{1,0:T(8,128)(2,1)} %get-tuple-element.31.b_ref, bf16[512,256]{1,0:T(8,128)(2,1)} %copy-done, ...), custom_call_target="tpu_custom_call" | custom-call | tf_op jit(solution)/shard_map/place/pallas_call | solution.py:635
Async XLA Ops:
  57.7 64.0 %collective-permute-start = (bf16[512,256]{1,0:T(8,128)(2,1)}, bf16[512,256]{1,0:T(8,128)(2,1)S(1)}, u32[]{:S(2)}, u32[]{:S(2)}) collective-permute-start(bf16[512,256]{1,0:T(8,128)(2,1)} %get-tuple-element.32), channel_id=1, source_target_pairs={{0,8},{1,9},{2,10},{3,11},{4,12},{5,13},{6,14},{7,15},{8,0},{9,1},... | collective-permute-start | bytes 786440 | tf_op jit(solution)/shard_map/ppermute | solution.py:657
  65.4 56.3 %collective-permute-start.1 = (bf16[512,256]{1,0:T(8,128)(2,1)}, bf16[512,256]{1,0:T(8,128)(2,1)S(1)}, u32[]{:S(2)}, u32[]{:S(2)}) collective-permute-start(bf16[512,256]{1,0:T(8,128)(2,1)} %get-tuple-element.33), channel_id=1, source_target_pairs={{0,9},{1,8},{2,11},{3,10},{4,13},{5,12},{6,15},{7,14},{8,1},{9,0},... | collective-permute-start | bytes 786440 | tf_op jit(solution)/shard_map/ppermute | solution.py:658
  121.7 0.7 copy-start
  121.7 0.8 copy-start.1
